TPU v7x, 32 devices: a whole 2x2x4 slice. The times are simulated.
32 devices in a mesh: dp: 8 (over y, x, core), pipe: 4 (over z).
Axes of the slice: x: 2, y: 2, z: 4, core: 2. Of those that a mesh axis runs over, the one named last changes fastest.
Arguments:
- tokens: bfloat16 [16, 2048, 256], P('dp', 'pipe'), may hold values from -6 to 6
- segments: int32 [16, 2048], P('dp'), may hold values from 0 to 7, never falling along the last dimension, each value on 1 to 512 neighbouring positions
- cotangent: bfloat16 [16, 2048, 256], P('dp', 'pipe'), may hold values from -6 to 6
- attention_in: bfloat16 [2, 256, 768], replicated, may hold values from -0.5 to 0.5
- attention_in_bias: float32 [2, 512], replicated, may hold values from -3 to 3
- attention_out: bfloat16 [2, 256, 256], replicated, may hold values from -1.5 to 1.5
- attention_out_bias: float32 [2, 256], replicated, may hold values from -2 to 2
- attention_gain: float32 [2, 256], replicated, may hold values from 0.25 to 1.75
- attention_shift: float32 [2, 256], replicated, may hold values from -2 to 2
- expand_weight: bfloat16 [2, 256, 512], replicated, may hold values from -0.375 to 0.375
- expand_bias: float32 [2, 512], replicated, may hold values from -3 to 3
- contract_weight: bfloat16 [2, 512, 256], replicated, may hold values from -0.375 to 0.375
- contract_bias: float32 [2, 256], replicated, may hold values from -2 to 2
- feed_gain: float32 [2, 256], replicated, may hold values from 0.25 to 1.75
- feed_shift: float32 [2, 256], replicated, may hold values from -2 to 2
Outputs:
- layer_output: bfloat16 [16, 2048, 256], P('dp', 'pipe')
- input_grad: bfloat16 [16, 2048, 256], P('dp', 'pipe')
- gradient_attention_in: float32 [2, 256, 768], replicated
- gradient_attention_in_bias: float32 [2, 512], replicated
- gradient_attention_out: float32 [2, 256, 256], replicated
- gradient_attention_out_bias: float32 [2, 256], replicated
- gradient_attention_gain: float32 [2, 256], replicated
- gradient_attention_shift: float32 [2, 256], replicated
- gradient_expand_weight: float32 [2, 256, 512], replicated
- gradient_expand_bias: float32 [2, 512], replicated
- gradient_contract_weight: float32 [2, 512, 256], replicated
- gradient_contract_bias: float32 [2, 256], replicated
- gradient_feed_gain: float32 [2, 256], replicated
- gradient_feed_shift: float32 [2, 256], replicated
Inputs may be any that keep to these rules, and one draw needn't show every extreme that they name: `segments`: along a row the numbers never fall; each of the 8 numbers marks one document of 1 to 512 consecutive positions, and some document has exactly 512.
All inputs are finite; a program needn't handle non-finite values.
Results may differ from a plain program's by a relative error of at most 0.03.
The roundings to bfloat16 on the way count: a program that leaves them out, or rounds other values in their place, can miss the bound.
Values may be sent and summed in bfloat16 or wider, within the bound.
No kernel may reach another device: no remote copies, remote signals or barrier semaphores. Data moves between devices by JAX's collectives and lax.ppermute only.
A program may use at most 192 MiB of HBM per device.

v0:
```python
from types import SimpleNamespace

import jax
import jax.numpy as jnp
from jax import lax
from jax.experimental import pallas as pl
from jax.experimental.pallas import tpu as pltpu
from jax.sharding import PartitionSpec as P

HEADS = 4
EPSILON = 1e-12
MASKED = -1e30
DOCS = 8
REACH = 320
TB = 512
MOST_BLOCKS = 8
QB = 128
LANES = 128

BF = jnp.bfloat16
F32 = jnp.float32

KEPT = dict(
    x=(256, BF),
    qkv=(768, BF),
    ctx=(256, BF),
    n1=(256, BF),
    r1=(128, F32),
    mid=(256, BF),
    act=(512, BF),
    slope=(512, BF),
    n2=(256, BF),
    r2=(128, F32),
)
NAMES = tuple(KEPT)


def dot(a, b):
    return jnp.dot(a, b, preferred_element_type=F32)


def dot_nt(a, b):
    return lax.dot_general(a, b, (((1,), (1,)), ((), ())), preferred_element_type=F32)


def dot_tn(a, b):
    return lax.dot_general(a, b, (((0,), (0,)), ((), ())), preferred_element_type=F32)


def fold(v):
    return v.reshape(-1, 8, v.shape[-1]).sum(0)


def rows_at(start, count):
    return pl.ds(pl.multiple_of(start, 16), count)


ITEMS = 2 * DOCS
ROOM = ITEMS + 1


class Plan:
    def __init__(self, r):
        self.table = r.table
        self.count, self.blocks, self.odd, self.end = (r.table[4 * ROOM + k] for k in range(4))

    def start(self, d):
        return self.table[d]

    def length(self, d):
        return self.table[ROOM + d]

    def offset(self, d):
        return self.table[2 * ROOM + d]

    def tile(self, d):
        return self.table[3 * ROOM + d]

    def size(self, d):
        return lax.shift_right_logical(self.length(d) + (QB - 1), 7)

    def over_docs(self, most, visit):
        def one(d, _):
            size = self.size(d)
            for n in range(1, most + 1):

                @pl.when(size == n)
                def _():
                    visit(d, n, self.length(d))

            return 0

        lax.fori_loop(0, self.count, one, 0)

    def over_groups(self, most, visit):
        def one(d):
            size = jnp.maximum(self.size(d), 2)
            after = self.size(d + 1)
            two = (size == 2) & (after >= 1) & (after <= 2)

            @pl.when(two)
            def _():
                visit([(d, 2), (d + 1, 2)])

            for n in range(2, most + 1):

                @pl.when((size == n) & jnp.logical_not(two))
                def _():
                    visit([(d, n)])

            return d + 1 + two.astype(jnp.int32)

        lax.while_loop(lambda d: d < self.count, one, jnp.int32(0))

    def over_blocks(self, visit):
        def one(b, _):
            visit(b, rows_at(b * TB, TB))
            return 0

        lax.fori_loop(0, self.blocks, one, 0)

        @pl.when(self.odd == 1)
        def _():
            visit(self.blocks, rows_at(self.blocks * TB, TB // 2))


def window_copies(win, span, own, low, high, sems, out):
    reach, whole = low.shape[1], own.shape[1]
    found = []
    for k in range(own.shape[0]):
        at = k * span
        for far, count in ((low, reach), (own, whole), (high, reach)):
            ends = (win.at[pl.ds(at, count)], far.at[k])
            found.append(pltpu.make_async_copy(*(ends if out else ends[::-1]), sems.at[len(found)]))
            at += count
    return found


def with_halos(r, win, span, act):
    upper = lax.bitwise_and(r.place[0], 1)
    for side in range(2):

        @pl.when(upper == 1 - side)
        def _():
            low, high = (r.odd, r.even) if side else (r.even, r.odd)
            act(window_copies(win, span, r.own, low, high, r.window_sems, False))


def clear_between(win, span, count):
    used = span - 2 * QB
    for k in range(count):
        clear(win, pl.ds(k * span + used, 2 * QB))


SPREAD = QB + 16


def pack(plan, most, win, dst):
    plan.over_blocks(lambda b, rows: clear(dst, rows))

    def visit(d, n, length):
        start, offset = plan.start(d), plan.offset(d)
        shift = lax.bitwise_and(start, 15)
        row = lax.broadcasted_iota(jnp.int32, (QB, SPREAD), 0)
        col = lax.broadcasted_iota(jnp.int32, (QB, SPREAD), 1)
        taken = col == row + shift
        kept = jnp.where(taken & (row < length - (n - 1) * QB), 1.0, 0.0).astype(BF)
        taken = jnp.where(taken, 1.0, 0.0).astype(BF)
        rows = [win[rows_at(start - shift + q * QB, SPREAD), :] for q in range(n)]
        picked = [dot(taken if q < n - 1 else kept, v).astype(BF) for q, v in enumerate(rows)]
        for q, v in enumerate(picked):
            dst[rows_at(offset + q * QB, QB), :] = v

    plan.over_docs(most, visit)


def unpack(plan, most, src, win, r, span, which):
    win[...] = jnp.zeros(win.shape, BF)
    clear(src, rows_at(plan.end, QB))

    def visit(d, n, length):
        start, offset = plan.start(d), plan.offset(d)
        shift = lax.bitwise_and(start, 15)
        row = lax.broadcasted_iota(jnp.int32, (SPREAD, QB), 0)
        col = lax.broadcasted_iota(jnp.int32, (SPREAD, QB), 1)
        taken = row == col + shift
        kept = jnp.where(taken & (col < length - (n - 1) * QB), 1.0, 0.0).astype(BF)
        taken = jnp.where(taken, 1.0, 0.0).astype(BF)
        rows = [src[rows_at(offset + q * QB, QB), :] for q in range(n)]
        placed = [dot(taken if q < n - 1 else kept, v) for q, v in enumerate(rows)]
        for q, v in enumerate(placed):
            at = rows_at(start - shift + q * QB, SPREAD)
            win[at, :] = (win[at, :].astype(F32) + v).astype(BF)

    plan.over_docs(most, visit)
    ends = [v.at[which] for v in (r.o_own, r.o_left, r.o_right)]
    found = window_copies(win, span, *ends, r.window_sems.at[which], True)
    started(found)
    return found


def clear(ref, rows):
    ref[rows, :] = jnp.zeros((rows.size, ref.shape[1]), ref.dtype)


def head_masks():
    lane = lax.broadcasted_iota(jnp.int32, (1, LANES), 1)
    low = (lane < LANES // 2).astype(F32)
    return low.astype(BF), (1.0 - low).astype(BF)


def two_heads(v, masks):
    return jnp.concatenate([v * masks[0], v * masks[1]], axis=0)


def turned_back(v):
    row = lax.broadcasted_iota(jnp.int32, (LANES, QB), 0)
    return jnp.where(row < LANES // 2, v[:, :QB], v[:, QB:]).T


def turn(src, dst, first, width):
    for k in range(width // LANES):
        at = slice(k * LANES, (k + 1) * LANES)
        for g in range(2):
            here = slice(g * LANES, (g + 1) * LANES)
            dst[here, first + at.start : first + at.stop] = src[at, here].T


def project(plan, kept, w, before=None):
    scaling = (256 // HEADS) ** (-0.5)
    bias = w.bin

    def visit(b, rows):
        if before is not None:
            before(b, rows)
        y = dot(kept.x[rows, :], w.win[...])
        queries = (y[:, 0:256] + bias[:, 0:256]).astype(BF)
        kept.qkv[rows, 0:256] = queries * jnp.asarray(scaling, BF)
        kept.qkv[rows, 256:512] = y[:, 256:512].astype(BF)
        kept.qkv[rows, 512:768] = (y[:, 512:768] + bias[:, 256:512]).astype(BF)
        clear(kept.ctx, rows)

    plan.over_blocks(visit)
    clear(kept.qkv, rows_at(plan.end, 2 * QB))


GROUPS = tuple(slice(g * LANES, (g + 1) * LANES) for g in range(2))


def shifted(cols, by):
    return slice(cols.start + by, cols.stop + by)


def attend(plan, most, kept, weights_low, values_turned):
    masks = head_masks()

    def visit(docs):
        offset = [plan.offset(d) for d, _ in docs]
        length = [plan.length(d) for d, _ in docs]
        tile = [plan.tile(d) for d, _ in docs]
        width = [n * QB for _, n in docs]
        firsts = [sum(width[:i]) for i in range(len(docs))]
        spans = [rows_at(o, v) for o, v in zip(offset, width)]
        for i, first in enumerate(firsts):
            turn(kept.qkv[spans[i], 512:768], values_turned, first, width[i])
        chains = [(i, q, g) for i, (_, n) in enumerate(docs) for q in range(n) for g in range(2)]
        column = lax.broadcasted_iota(jnp.int32, (1, 2 * QB), 1)
        column = lax.bitwise_and(column, QB - 1)
        row = lax.broadcasted_iota(jnp.int32, (QB, 2 * QB), 0)
        keys = [[kept.qkv[at, shifted(c, 256)] for c in GROUPS] for at in spans]
        turned = [[values_turned[c, f : f + v] for c in GROUPS] for f, v in zip(firsts, width)]
        queries = [kept.qkv[rows_at(offset[i] + q * QB, QB), GROUPS[g]] for i, q, g in chains]
        queries = [two_heads(v, masks) for v in queries]
        scores = [dot_nt(keys[i][g], v) for v, (i, _, g) in zip(queries, chains)]
        probs = []
        for v, (i, q, g) in zip(scores, chains):
            parts = []
            for k in range(docs[i][1]):
                part = v[k * QB : (k + 1) * QB, :]
                if k == docs[i][1] - 1 or docs[i][1] == 2:
                    part = jnp.where(row < length[i] - k * QB, part, MASKED)
                parts.append(part)
            v = jnp.concatenate(parts, axis=0)
            raised = jnp.exp(v - jnp.max(v, axis=0, keepdims=True))
            total = jnp.sum(raised, axis=0, keepdims=True)
            share = jnp.where(column < length[i] - q * QB, 1.0 / total, 0.0)
            probs.append((raised * share).astype(BF))
        contexts = [dot(turned[i][g], v) for v, (i, _, g) in zip(probs, chains)]
        contexts = [turned_back(v).astype(BF) for v in contexts]
        for v, context, (i, q, g) in zip(probs, contexts, chains):
            kept.ctx[rows_at(offset[i] + q * QB, QB), GROUPS[g]] = context
            n = docs[i][1]
            for k in range(n):
                weights_low[tile[i] + q * n + k, g] = v[k * QB : (k + 1) * QB, :]

    plan.over_groups(most, visit)


def normal(v):
    centred = v - jnp.mean(v, axis=1, keepdims=True)
    spread = jnp.mean(centred * centred, axis=1, keepdims=True)
    rate = lax.rsqrt(spread + EPSILON)
    return centred * rate, rate


def parts_of(rows, count):
    step = rows.size // count
    return [rows_at(rows.start + k * step, step) for k in range(count)]


def feed(plan, kept, w, out, each=None):
    def visit(b, rows):
        chains = parts_of(rows, 1)
        wout, wup, wdown = w.wout[...], w.wup[...], w.wdown[...]
        x = [kept.x[at, :] for at in chains]
        ctx = [kept.ctx[at, :] for at in chains]
        attn_sum = [u.astype(F32) + dot(v, wout) + w.bout for u, v in zip(x, ctx)]
        first = [normal(v) for v in attn_sum]
        mid_low = [(n * w.g1 + w.s1).astype(BF) for n, _ in first]
        pre_up = [dot(v, wup) + w.bup for v in mid_low]
        share = [0.5 + 0.5 * lax.erf(v * (0.5**0.5)) for v in pre_up]
        active = [(v * p).astype(BF) for v, p in zip(pre_up, share)]
        density = [jnp.exp(v * v * -0.5) * 0.3989422804014327 for v in pre_up]
        slope = [(p + v * q).astype(BF) for v, p, q in zip(pre_up, share, density)]
        feed_sum = [u.astype(F32) + dot(v, wdown) + w.bdown for u, v in zip(mid_low, active)]
        second = [normal(v) for v in feed_sum]
        for k, at in enumerate(chains):
            kept.n1[at, :] = first[k][0].astype(BF)
            kept.r1[at, :] = jnp.broadcast_to(first[k][1], (at.size, LANES))
            kept.mid[at, :] = mid_low[k]
            kept.act[at, :] = active[k]
            kept.slope[at, :] = slope[k]
            kept.n2[at, :] = second[k][0].astype(BF)
            kept.r2[at, :] = jnp.broadcast_to(second[k][1], (at.size, LANES))
            out[at, :] = (second[k][0] * w.g2 + w.s2).astype(BF)
        if each is not None:
            each(b, rows)

    plan.over_blocks(visit)


AT_OUT, AT_UP, AT_DOWN, AT_ALL = 768, 1024, 1536, 2048
V_IN, V_OUT, V_G1, V_S1, V_UP, V_DOWN, V_G2, V_S2, V_ALL = 0, 2, 3, 4, 5, 7, 8, 9, 16


def norm_back(upstream, n, rate, gain):
    e = upstream * gain
    inner = jnp.mean(e * n, axis=1, keepdims=True)
    return (e - jnp.mean(e, axis=1, keepdims=True) - n * inner) * rate


def doubled(v):
    return jnp.concatenate([v, v], axis=1)


def joined(values):
    return jnp.concatenate(values, axis=0) if len(values) > 1 else values[0]


def feed_back(plan, kept, w, upstream, r, before=None):
    total, small, ctx_grad, sum_grad = r.s_total, r.s_small, r.s_ctx_grad, r.s_sum_grad

    def visit(b, rows):
        if before is not None:
            before(b, rows)
        chains = parts_of(rows, 2)
        wout, wup, wdown = w.wout[...], w.wup[...], w.wdown[...]
        up = [upstream[at, :].astype(F32) for at in chains]
        n2 = [kept.n2[at, :].astype(F32) for at in chains]
        r2 = [doubled(kept.r2[at, :]) for at in chains]
        slope = [kept.slope[at, :] for at in chains]
        n1 = [kept.n1[at, :].astype(F32) for at in chains]
        r1 = [doubled(kept.r1[at, :]) for at in chains]
        act, mid, ctx = kept.act[rows, :], kept.mid[rows, :], kept.ctx[rows, :]
        feed_grad = [norm_back(u, n, v, w.g2) for u, n, v in zip(up, n2, r2)]
        feed_low = [v.astype(BF) for v in feed_grad]
        active_grad = [dot_nt(v, wdown) for v in feed_low]
        pre_grad = [(v * p.astype(F32)).astype(BF) for v, p in zip(active_grad, slope)]
        mid_grad = [dot_nt(v, wup) + u for v, u in zip(pre_grad, feed_grad)]
        mid_grad = [v.astype(BF).astype(F32) for v in mid_grad]
        attn_grad = [norm_back(u, n, v, w.g1) for u, n, v in zip(mid_grad, n1, r1)]
        attn_low = [v.astype(BF) for v in attn_grad]
        back = [dot_nt(v, wout).astype(BF) for v in attn_low]
        down_total = dot_tn(act, joined(feed_low))
        up_total = dot_tn(mid, joined(pre_grad))
        out_total = dot_tn(ctx, joined(attn_low))
        up_sums = fold(joined(pre_grad).astype(F32))
        sums = [
            (V_G2, fold(joined([u * n for u, n in zip(up, n2)]))),
            (V_S2, fold(joined(up))),
            (V_DOWN, fold(joined(feed_low).astype(F32))),
            (V_UP, up_sums[:, :256]),
            (V_UP + 1, up_sums[:, 256:]),
            (V_G1, fold(joined([u * n for u, n in zip(mid_grad, n1)]))),
            (V_S1, fold(joined(mid_grad))),
            (V_OUT, fold(joined(attn_low).astype(F32))),
        ]
        for k, at in enumerate(chains):
            sum_grad[at, :] = attn_grad[k]
            ctx_grad[at, :] = back[k]
        total[AT_DOWN:AT_ALL, :] += down_total
        total[AT_UP : AT_UP + 256, :] += up_total[:, :256]
        total[AT_UP + 256 : AT_DOWN, :] += up_total[:, 256:]
        total[AT_OUT:AT_UP, :] += out_total
        for line, v in sums:
            small[line] += v

    plan.over_blocks(visit)
    clear(ctx_grad, rows_at(plan.end, 2 * QB))


def attend_back(plan, most, kept, r):
    weights_low, ctx_grad, qkv_grad, keys_turned = r.s_probs, r.s_ctx_grad, r.s_qkv_grad, r.s_turned
    masks = head_masks()
    scaling = (256 // HEADS) ** (-0.5)
    plan.over_blocks(lambda b, rows: clear(qkv_grad, rows))

    def visit(docs):
        offset = [plan.offset(d) for d, _ in docs]
        tile = [plan.tile(d) for d, _ in docs]
        width = [n * QB for _, n in docs]
        firsts = [sum(width[:i]) for i in range(len(docs))]
        spans = [rows_at(o, v) for o, v in zip(offset, width)]
        for i, first in enumerate(firsts):
            turn(kept.qkv[spans[i], 256:512], keys_turned, first, width[i])
        chains = [(i, q, g) for i, (_, n) in enumerate(docs) for q in range(n) for g in range(2)]
        values = [[kept.qkv[at, shifted(c, 512)] for c in GROUPS] for at in spans]
        turned = [[keys_turned[c, f : f + v] for c in GROUPS] for f, v in zip(firsts, width)]
        queries = [kept.qkv[rows_at(offset[i] + q * QB, QB), GROUPS[g]] for i, q, g in chains]
        grads = [ctx_grad[rows_at(offset[i] + q * QB, QB), GROUPS[g]] for i, q, g in chains]
        probs = []
        for i, q, g in chains:
            n = docs[i][1]
            probs.append(joined([weights_low[tile[i] + q * n + k, g] for k in range(n)]))
        queries = [two_heads(v, masks) for v in queries]
        grads = [two_heads(v, masks) for v in grads]
        prob_grads = [dot_nt(values[i][g], v) for v, (i, _, g) in zip(grads, chains)]
        score_grads = []
        for low, v in zip(probs, prob_grads):
            full = low.astype(F32)
            inner = jnp.sum(full * v, axis=0, keepdims=True)
            score_grads.append((full * (v - inner)).astype(BF))
        query_grads = [dot(turned[i][g], v) for v, (i, _, g) in zip(score_grads, chains)]
        query_grads = [(turned_back(v) * scaling).astype(BF) for v in query_grads]
        sums = []
        for i in range(len(docs)):
            for g in range(2):
                mine = [k for k, c in enumerate(chains) if (c[0], c[2]) == (i, g)]
                sides = jnp.concatenate([score_grads[k] for k in mine], axis=1)
                key_sum = dot(sides, joined([queries[k] for k in mine])).astype(BF)
                sides = jnp.concatenate([probs[k] for k in mine], axis=1)
                value_sum = dot(sides, joined([grads[k] for k in mine])).astype(BF)
                sums.append((i, g, key_sum, value_sum))
        for i in range(len(docs)):
            for v, (own, q, g) in zip(query_grads, chains):
                if own == i:
                    qkv_grad[rows_at(offset[i] + q * QB, QB), GROUPS[g]] = v
            for own, g, key_sum, value_sum in sums:
                if own == i:
                    qkv_grad[spans[i], shifted(GROUPS[g], 256)] = key_sum
                    qkv_grad[spans[i], shifted(GROUPS[g], 512)] = value_sum

    plan.over_groups(most, visit)


def project_back(plan, kept, w, r, out, after=None):
    qkv_grad, sum_grad, total, small = r.s_qkv_grad, r.s_sum_grad, r.s_total, r.s_small

    def visit(b, rows):
        grad = qkv_grad[rows, :]
        sums = fold(grad.astype(F32))
        small[V_IN] += sums[:, :256]
        small[V_IN + 1] += sums[:, 512:]
        in_grad = dot_tn(kept.x[rows, :], grad)
        for k in range(3):
            total[256 * k : 256 * (k + 1), :] += in_grad[:, 256 * k : 256 * (k + 1)]
        hidden_grad = dot_nt(grad, w.win[...]) + sum_grad[rows, :]
        out[rows, :] = hidden_grad.astype(BF)
        if after is not None:
            after(b, rows)

    plan.over_blocks(visit)


def copies(r, kept, plan, out):
    def one(name, rows, sem):
        near = getattr(r if name == "probs" else kept, "s_probs" if name == "probs" else name)
        far = getattr(r, ("o_" if out else "i_") + name)
        ends = (near.at[rows], far.at[rows])
        return pltpu.make_async_copy(*(ends if out else ends[::-1]), sem)

    def of_block(names, b, rows):
        return [one(k, rows, r.sems.at[NAMES.index(k), b]) for k in names]

    def of_doc(d, n):
        return one("probs", pl.ds(plan.tile(d), max(n, 2) ** 2), r.sems.at[len(NAMES), 0])

    return of_block, of_doc


def by_block(source, target, sems):
    return lambda b, rows: [pltpu.make_async_copy(source.at[rows], target.at[rows], sems.at[b])]


def started(found):
    for c in found:
        c.start()


def waited(found):
    for c in found:
        c.wait()


def first_kernel(most, span, r):
    with_halos(r, r.s_window, span, started)
    w = layer_of(r, 0)
    plan = Plan(r)
    kept = SimpleNamespace(**{k: getattr(r, "s_" + k) for k in NAMES})
    of_block, of_doc = copies(r, kept, plan, True)
    leaving = by_block(r.s_rows, r.o_next, r.out_sems)
    clear_between(r.s_window, span, r.own.shape[0])
    with_halos(r, r.s_window, span, waited)
    pack(plan, most, r.s_window, kept.x)
    waited(w.coming)
    project(plan, kept, w)
    early, late = NAMES[:2], NAMES[2:]
    plan.over_blocks(lambda b, rows: started(of_block(early, b, rows)))
    attend(plan, most, kept, r.s_probs, r.s_turned)
    plan.over_docs(most, lambda d, n, length: of_doc(d, n).start())
    feed(plan, kept, w, r.s_rows, lambda b, rows: started(leaving(b, rows) + of_block(late, b, rows)))
    plan.over_blocks(lambda b, rows: waited(leaving(b, rows) + of_block(NAMES, b, rows)))
    plan.over_docs(most, lambda d, n, length: of_doc(d, n).wait())


def second_kernel(most, span, r):
    plan = Plan(r)
    kept = SimpleNamespace(**{k: getattr(r, "s_" + k) for k in NAMES})
    coming = by_block(r.x, kept.x, r.in_sems)
    plan.over_blocks(lambda b, rows: started(coming(b, rows)))
    w = layer_of(r, 1)
    with_halos(r, r.s_window, span, started)
    below = layer_of(r, 0)
    waited(w.coming)
    project(plan, kept, w, lambda b, rows: waited(coming(b, rows)))
    attend(plan, most, kept, r.s_probs, r.s_turned)
    leaving = by_block(r.s_ctx_grad, r.o_out, r.out_sems)
    feed(plan, kept, w, r.s_ctx_grad, lambda b, rows: started(leaving(b, rows)))
    clear_between(r.s_window, span, r.own.shape[0])
    with_halos(r, r.s_window, span, waited)
    pack(plan, most, r.s_window, r.s_rows)
    plan.over_blocks(lambda b, rows: waited(leaving(b, rows)))
    of_block, of_doc = copies(r, kept, plan, False)
    fed, projected, given = NAMES[2:], NAMES[1:2], NAMES[:1]
    waited(below.coming)
    leaving = by_block(r.s_rows, r.o_grad, r.out_sems)

    def one(step, _):
        w = weights_of(r, 1 - step)

        def at(which, act):
            pl.when(step == which)(act)

        def come(names, act):
            plan.over_blocks(lambda b, rows: act(of_block(names, b, rows)))

        def before(b, rows):
            at(1, lambda: waited(of_block(fed, b, rows)))

        def after(b, rows):
            at(1, lambda: started(leaving(b, rows)))

        clear_totals(r)
        feed_back(plan, kept, w, r.s_rows, r, before)
        at(0, lambda: come(fed, started))

        @pl.when(step == 1)
        def _():
            plan.over_docs(most, lambda d, n, length: of_doc(d, n).wait())
            come(projected, waited)

        attend_back(plan, most, kept, r)

        @pl.when(step == 0)
        def _():
            plan.over_docs(most, lambda d, n, length: of_doc(d, n).start())
            come(projected, started)

        at(1, lambda: come(given, waited))
        project_back(plan, kept, w, r, r.s_rows, after)
        at(0, lambda: come(given, started))
        r.s_both[pl.ds(pl.multiple_of((1 - step) * V_ALL, V_ALL), V_ALL), :] = r.s_small[...].sum(1)
        at(0, lambda: send_pieces(r, r.o_keep1, r.o_send1, r.self[1]))
        at(1, lambda: send_pieces(r, r.o_keep0, r.o_send0, r.self[0]))
        return 0

    lax.fori_loop(0, 2, one, 0)
    send_small(r, r.o_keep0, r.o_send0, r.self[0])
    plan.over_blocks(lambda b, rows: waited(leaving(b, rows)))


def third_kernel(most, span, r):
    plan = Plan(r)
    coming = [by_block(r.out, r.s_rows, r.in_sems), by_block(r.grad, r.s_sent, r.out_sems)]
    for one in coming:
        plan.over_blocks(lambda b, rows: started(one(b, rows)))
    found = []
    for k, (one, rows) in enumerate(zip(coming, (r.s_rows, r.s_sent))):
        plan.over_blocks(lambda b, at: waited(one(b, at)))
        found += unpack(plan, most, rows, r.s_window.at[k], r, span, k)
    waited(found)


VECTORS = dict(bin=512, bout=256, g1=256, s1=256, bup=512, bdown=256, g2=256, s2=256)


def weights_of(r, layer):
    near = dict(win=r.s_win, wout=r.s_wout, wup=r.s_wup, wdown=r.s_wdown)
    near = {k: v.at[layer] for k, v in near.items()}
    vectors = {k: r.s_vectors[layer, i : i + 1, 0:n] for i, (k, n) in enumerate(VECTORS.items())}
    return SimpleNamespace(**near, **vectors)


def layer_of(r, layer):
    pairs = ((r.win, r.s_win), (r.wout, r.s_wout), (r.wup, r.s_wup), (r.wdown, r.s_wdown))
    coming = []
    for k, (far, near) in enumerate(pairs):
        sem = r.weight_sems.at[4 * layer + k]
        coming.append(pltpu.make_async_copy(far.at[layer], near.at[layer], sem))
    started(coming)
    for i, (k, n) in enumerate(VECTORS.items()):
        r.s_vectors[layer, i : i + 1, 0:n] = getattr(r, k)[layer : layer + 1, :]
    w = weights_of(r, layer)
    w.coming = coming
    return w


def clear_totals(r):
    r.s_total[...] = jnp.zeros(r.s_total.shape, F32)
    r.s_small[...] = jnp.zeros(r.s_small.shape, F32)


def send_pieces(r, keep, send, own):
    half = keep.shape[0]
    rows = AT_ALL // (2 * half)
    for p in range(2 * half):
        out = keep if p < half else send
        at = pl.ds(pl.multiple_of(lax.bitwise_xor(jnp.int32(p), own) * rows, rows), rows)
        out[p % half, 0:rows, :] = r.s_total[at, :].astype(BF)


def send_small(r, keep, send, own):
    half = keep.shape[0]
    rows = AT_ALL // (2 * half)
    extra = keep.shape[1] - rows
    share = V_ALL // half
    for j in range(2 * half):
        line = r.s_both[j * share : (j + 1) * share, :]
        r.s_spread[j] = jnp.concatenate([line, jnp.zeros((extra - share, line.shape[1]), F32)], axis=0)
    for p in range(2 * half):
        out = keep if p < half else send
        out[p % half, rows : rows + extra, :] = r.s_spread[lax.bitwise_xor(jnp.int32(p), own)].astype(BF)


def last_kernel(r):
    half = r.keep0.shape[0]
    count = 2 * half
    rows = AT_ALL // count
    share = 2 * V_ALL // count
    big = (
        (0, AT_OUT, r.s_in, r.o_in),
        (AT_OUT, AT_UP, r.s_out, r.o_out),
        (AT_UP, AT_DOWN, r.s_up, r.o_up),
        (AT_DOWN, AT_ALL, r.s_down, r.o_down),
    )
    sent = []
    for layer, (keep, got) in enumerate(((r.keep0, r.got0), (r.keep1, r.got1))):
        for p in range(count):
            piece = lax.bitwise_xor(jnp.int32(p), r.self[layer])
            source = keep if p < half else got
            r.s_pieces[layer, piece, 0 : keep.shape[1], :] = source[p % half]
        for low, high, near, far in big:
            tall = near.shape[1]
            for at in range(low, high, rows):
                line, col = (at - low) % tall, (at - low) // tall * 256
                value = r.s_pieces[layer, at // rows, 0:rows, :].astype(F32)
                near[layer, line : line + rows, col : col + 256] = value
            copy = pltpu.make_async_copy(near.at[layer], far.at[layer], r.sems.at[len(sent)])
            copy.start()
            sent.append(copy)
    for j in range(count):
        tail = r.s_pieces[0, j, rows : rows + 16, :].astype(F32)
        r.s_both[j * share : (j + 1) * share, :] = tail[0:share]
    for layer in range(2):
        at = layer * V_ALL
        here = pl.ds(layer, 1)

        def line(k):
            return r.s_both[at + k : at + k + 1, :]

        r.o_bin[here, :] = jnp.concatenate([line(V_IN), line(V_IN + 1)], axis=1)
        r.o_bout[here, :] = line(V_OUT)
        r.o_g1[here, :] = line(V_G1)
        r.o_s1[here, :] = line(V_S1)
        r.o_bup[here, :] = jnp.concatenate([line(V_UP), line(V_UP + 1)], axis=1)
        r.o_bdown[here, :] = line(V_DOWN)
        r.o_g2[here, :] = line(V_G2)
        r.o_s2[here, :] = line(V_S2)
    waited(sent)


def call(kernel, consts, inputs, outputs, scratch, flops, megabytes):
    names = tuple(inputs) + tuple(outputs) + tuple(scratch)

    def run(*refs):
        kernel(*consts, SimpleNamespace(**dict(zip(names, refs))))

    got = pl.pallas_call(
        run,
        out_shape=[jax.ShapeDtypeStruct(s, d) for s, d, _ in outputs.values()],
        in_specs=[spec for _, spec in inputs.values()],
        out_specs=[spec for _, _, spec in outputs.values()],
        scratch_shapes=list(scratch.values()),
        compiler_params=pltpu.CompilerParams(vmem_limit_bytes=megabytes << 20),
        cost_estimate=pl.CostEstimate(flops=flops, bytes_accessed=8 << 20, transcendentals=0),
    )(*[a for a, _ in inputs.values()])
    return SimpleNamespace(**dict(zip(outputs, got)))


def plan_kernel(sections, whole, span, r):
    base = DOCS + 1
    huge = jnp.int32(1 << 20)
    for row in range(2):
        line = r.segments[row : row + 1, :]
        starts = [jnp.int32(0)]
        for doc in range(1, DOCS):
            below = jnp.where(line < doc, 1.0, 0.0)
            starts.append(jnp.sum(below).astype(jnp.int32))
        starts.append(jnp.int32(sections * whole))
        spent = jnp.int32(0)
        for doc in range(base):
            r.start[row * base + doc] = starts[doc]
            r.spent[row * base + doc] = spent
            if doc < DOCS:
                size = starts[doc + 1] - starts[doc]
                spent = spent + size + 230
                spent = spent + jnp.where(size > 2 * QB, 270, 0) + jnp.where(size > 3 * QB, 330, 0)
        for section in range(1, sections):
            low, high = jnp.int32(0), jnp.int32(0)
            for doc in range(base):
                away = starts[doc] - section * whole
                low = low + (away < -REACH).astype(jnp.int32)
                high = high + (away <= REACH).astype(jnp.int32)
            r.low[2 * section + row] = low
            r.high[2 * section + row] = high

    def over(section, visit, first):
        def outer(i, carry):
            inner = lambda j, c: visit(i, j, c)
            return lax.fori_loop(r.low[2 * section + 1], r.high[2 * section + 1], inner, carry)

        return lax.fori_loop(r.low[2 * section], r.high[2 * section], outer, first)

    def least(section, end, top, right):
        def visit(i, j, carry):
            cost, code = carry
            at = i * base + j
            step = end - r.spent[i] - r.spent[base + j]
            new = jnp.maximum(r.best[section * base * base + at], step)
            new = jnp.where((i <= top) & (j <= right), new, huge)
            better = new < cost
            return jnp.where(better, new, cost), jnp.where(better, at, code)

        return over(section, visit, (huge, jnp.int32(0)))

    for section in range(1, sections):

        def visit(i, j, carry):
            at = section * base * base + i * base + j
            end = r.spent[i] + r.spent[base + j]
            if section == 1:
                r.best[at] = end
            else:
                r.best[at], r.way[at] = least(section - 1, end, i, j)
            return carry

        over(section, visit, jnp.int32(0))
    _, code = least(sections - 1, r.spent[DOCS] + r.spent[base + DOCS], jnp.int32(DOCS), jnp.int32(DOCS))
    cuts = [jnp.int32(base * base - 1), code]
    for section in range(sections - 1, 1, -1):
        code = r.way[section * base * base + code]
        cuts.append(code)
    cuts = (cuts + [jnp.int32(0)])[::-1]
    place = r.place[0]
    low, high = jnp.int32(0), jnp.int32(0)
    for section in range(sections):
        low = jnp.where(place == section, cuts[section], low)
        high = jnp.where(place == section, cuts[section + 1], high)
    low, high = (low // base, low % base), (high // base, high % base)
    k, offset, tile = jnp.int32(0), jnp.int32(0), jnp.int32(0)
    table = r.table
    for row in range(2):

        def one(doc, carry):
            k, offset, tile = carry
            begin = r.start[row * base + doc]
            length = r.start[row * base + doc + 1] - begin
            table[k] = begin - place * whole + REACH + row * span
            table[ROOM + k] = length
            table[2 * ROOM + k] = offset
            table[3 * ROOM + k] = tile
            blocks = jnp.maximum(lax.shift_right_logical(length + (QB - 1), 7), 2)
            return k + 1, offset + lax.bitwise_and(length + 15, -16), tile + blocks * blocks

        k, offset, tile = lax.fori_loop(low[row], high[row], one, (k, offset, tile))
    table[ROOM + k] = 0
    halves = lax.shift_right_logical(offset + (TB // 2 - 1), 8)
    table[4 * ROOM] = k
    table[4 * ROOM + 1] = lax.shift_right_logical(halves, 1)
    table[4 * ROOM + 2] = lax.bitwise_and(halves, 1)
    table[4 * ROOM + 3] = halves * (TB // 2)


def halo_sent(low_part, high_part, place):
    upper = lax.rem(place, 2) == 1
    return jnp.where(upper, low_part, high_part), jnp.where(upper, high_part, low_part)


def halo(sent):
    count = lax.axis_size("pipe")
    got = []
    for odd, value in enumerate(sent):
        pairs = [(i, i + 1) for i in range(odd, count - 1, 2)]
        got.append(lax.ppermute(value, "pipe", [p for i, j in pairs for p in ((i, j), (j, i))]))
    return got


def orders():
    found = []
    for axis in ("dp", "pipe"):
        stride = 1
        while stride < lax.axis_size(axis):
            found.append((axis, stride))
            stride *= 2
    other = list(found)
    if len(found) > 2:
        other[1], other[2] = found[2], found[1]
    return found, other


SPLIT = 4


def self_index(order):
    index = jnp.int32(0)
    for axis, stride in order[:SPLIT]:
        index = 2 * index + lax.rem(lax.div(lax.axis_index(axis), stride), 2)
    return index.astype(jnp.int32)


def exchange(value, axis, stride):
    count = lax.axis_size(axis)
    return lax.ppermute(value, axis, [(i, i ^ stride) for i in range(count)])


def added(a, b):
    return (a.astype(F32) + b.astype(F32)).astype(BF)


def sum_steps(keep, send, order):
    total = None
    for k, (axis, stride) in enumerate(order[:SPLIT]):
        got = exchange(send, axis, stride)
        yield None
        half = keep.shape[0] // 2
        if half:
            send, keep = added(keep[half:], got[half:]), added(keep[:half], got[:half])
        else:
            total = added(keep, got)
    for axis, stride in order[SPLIT:]:
        got = exchange(total, axis, stride)
        yield None
        total = added(total, got)
    for k, (axis, stride) in enumerate(reversed(order[:SPLIT])):
        got = exchange(total, axis, stride)
        yield (total, got)
        total = jnp.concatenate([total, got], axis=0)


def body(
    tokens,
    segments,
    cotangent,
    attention_in,
    attention_in_bias,
    attention_out,
    attention_out_bias,
    attention_gain,
    attention_shift,
    expand_weight,
    expand_bias,
    contract_weight,
    contract_bias,
    feed_gain,
    feed_shift,
):
    section_count = lax.axis_size("pipe")
    place = lax.axis_index("pipe").astype(jnp.int32)
    row_count, whole, features = tokens.shape
    span = whole + 2 * REACH + 2 * QB
    most = whole // QB
    cap = row_count * (whole + 2 * REACH) + ITEMS * 15
    cap = (cap + TB // 2 - 1) // (TB // 2) * (TB // 2) + 2 * QB
    tiles = row_count * 53
    vmem = pl.BlockSpec(memory_space=pltpu.VMEM)
    smem = pl.BlockSpec(memory_space=pltpu.SMEM)
    hbm = pl.BlockSpec(memory_space=pltpu.HBM)
    anywhere = pl.BlockSpec(memory_space=pl.ANY)
    weights = dict(
        win=attention_in,
        bin=attention_in_bias,
        wout=attention_out,
        bout=attention_out_bias,
        g1=attention_gain,
        s1=attention_shift,
        wup=expand_weight,
        bup=expand_bias,
        wdown=contract_weight,
        bdown=contract_bias,
        g2=feed_gain,
        s2=feed_shift,
    )
    weights = {k: (v, vmem if v.ndim == 2 else hbm) for k, v in weights.items()}
    weight_scratch = dict(
        s_win=pltpu.VMEM(attention_in.shape, BF),
        s_wout=pltpu.VMEM(attention_out.shape, BF),
        s_wup=pltpu.VMEM(expand_weight.shape, BF),
        s_wdown=pltpu.VMEM(contract_weight.shape, BF),
        s_vectors=pltpu.VMEM((attention_in.shape[0], len(VECTORS), 2 * features), F32),
        weight_sems=pltpu.SemaphoreType.DMA((4 * attention_in.shape[0],)),
    )

    order0, order1 = orders()
    selves = [self_index(order0), self_index(order1)]
    pieces = 1 << SPLIT
    even, odd = halo(halo_sent(tokens[:, :REACH], tokens[:, whole - REACH :], place))
    token_rows = dict(own=(tokens, anywhere), even=(even, anywhere), odd=(odd, anywhere))
    choices = section_count * (DOCS + 1) ** 2
    planned = call(
        plan_kernel,
        (section_count, whole, span),
        dict(segments=(segments, vmem), place=(place.reshape(1), smem)),
        dict(table=((4 * ROOM + 4,), jnp.int32, smem)),
        dict(
            start=pltpu.SMEM((2 * (DOCS + 1),), jnp.int32),
            spent=pltpu.SMEM((2 * (DOCS + 1),), jnp.int32),
            low=pltpu.SMEM((2 * section_count,), jnp.int32),
            high=pltpu.SMEM((2 * section_count,), jnp.int32),
            best=pltpu.SMEM((choices,), jnp.int32),
            way=pltpu.SMEM((choices,), jnp.int32),
        ),
        1 << 20,
        4,
    )
    plan = dict(table=(planned.table, smem), place=(place.reshape(1), smem))
    sent = halo_sent(cotangent[:, :REACH], cotangent[:, whole - REACH :], place)
    even, odd = halo(lax.optimization_barrier((*sent, planned.table))[:2])
    cotangent_rows = dict(own=(cotangent, anywhere), even=(even, anywhere), odd=(odd, anywhere))
    kept_scratch = {"s_" + k: pltpu.VMEM((cap, c), t) for k, (c, t) in KEPT.items()}
    kept_scratch.update(weight_scratch)
    probs_shape = (tiles, 2, QB, 2 * QB)
    kept_scratch.update(
        s_probs=pltpu.VMEM(probs_shape, BF),
        s_window=pltpu.VMEM((row_count * span, features), BF),
        s_turned=pltpu.VMEM((features, whole), BF),
    )
    sems = dict(sems=pltpu.SemaphoreType.DMA((len(NAMES) + 1, MOST_BLOCKS)))
    moved = dict(
        s_rows=pltpu.VMEM((cap, features), BF),
        window_sems=pltpu.SemaphoreType.DMA((3 * row_count,)),
        in_sems=pltpu.SemaphoreType.DMA((MOST_BLOCKS,)),
        out_sems=pltpu.SemaphoreType.DMA((MOST_BLOCKS,)),
    )
    back_scratch = dict(
        s_total=pltpu.VMEM((AT_ALL, features), F32),
        s_small=pltpu.VMEM((V_ALL, 8, features), F32),
        s_ctx_grad=pltpu.VMEM((cap, features), BF),
        s_sum_grad=pltpu.VMEM((cap, features), F32),
        s_qkv_grad=pltpu.VMEM((cap, 3 * features), BF),
    )
    def pieces_out(extra):
        return ((pieces // 2, AT_ALL // pieces + extra, features), BF, vmem)

    rows_out = ((cap, features), BF, hbm)
    kept_out = {"o_" + k: ((cap, c), t, hbm) for k, (c, t) in KEPT.items()}
    kept_out.update(o_probs=(probs_shape, BF, hbm), o_next=rows_out)
    shape = (most, span)

    first = call(
        first_kernel,
        shape,
        plan | token_rows | weights,
        kept_out,
        kept_scratch | sems | moved,
        12 << 30,
        60,
    )
    kept_in = {"i_" + k: (getattr(first, "o_" + k), hbm) for k in NAMES + ("probs",)}
    second = call(
        second_kernel,
        shape,
        plan
        | cotangent_rows
        | kept_in
        | dict(x=(first.o_next, hbm), self=(jnp.stack(selves), smem))
        | weights,
        dict(
            o_keep0=pieces_out(16),
            o_send0=pieces_out(16),
            o_keep1=pieces_out(0),
            o_send1=pieces_out(0),
            o_out=rows_out,
            o_grad=rows_out,
        ),
        kept_scratch
        | back_scratch
        | sems
        | moved
        | dict(
            s_both=pltpu.VMEM((2 * V_ALL, features), F32),
            s_spread=pltpu.VMEM((pieces, 16, features), F32),
        ),
        60 << 30,
        57,
    )
    sums = [sum_steps(second.o_keep0, second.o_send0, order0)]
    sums.append(sum_steps(second.o_keep1, second.o_send1, order1))
    third = call(
        third_kernel,
        shape,
        plan | dict(out=(second.o_out, hbm), grad=(second.o_grad, hbm)),
        dict(
            o_own=((2, row_count, whole, features), BF, anywhere),
            o_left=((2, row_count, REACH, features), BF, anywhere),
            o_right=((2, row_count, REACH, features), BF, anywhere),
        ),
        moved
        | dict(
            s_sent=pltpu.VMEM((cap, features), BF),
            s_window=pltpu.VMEM((2, row_count * span, features), BF),
                window_sems=pltpu.SemaphoreType.DMA((2, 3 * row_count)),
        ),
        2 << 30,
        20,
    )
    even, odd = halo(halo_sent(third.o_left, third.o_right, place))
    upper = lax.rem(place, 2) == 1
    gap = jnp.zeros((2, row_count, whole - REACH, features), BF)
    low = jnp.concatenate([jnp.where(upper, even, odd), gap], axis=2)
    high = jnp.concatenate([gap, jnp.where(upper, odd, even)], axis=2)
    layer_output, input_grad = [third.o_own[k] + low[k] + high[k] for k in range(2)]
    for ends in zip(*sums):
        pass
    layers = attention_in.shape[0]

    def out(*shape):
        return ((layers,) + shape, F32, hbm)

    def small_out(*shape):
        return ((layers,) + shape, F32, vmem)

    vector = small_out(features)
    result = call(
        last_kernel,
        (),
        dict(
            self=(jnp.stack(selves), smem),
            keep0=(ends[0][0], vmem),
            got0=(ends[0][1], vmem),
            keep1=(ends[1][0], vmem),
            got1=(ends[1][1], vmem),
        ),
        dict(
            o_in=out(features, 3 * features),
            o_bin=small_out(2 * features),
            o_out=out(features, features),
            o_bout=vector,
            o_g1=vector,
            o_s1=vector,
            o_up=out(features, 2 * features),
            o_bup=small_out(2 * features),
            o_down=out(2 * features, features),
            o_bdown=vector,
            o_g2=vector,
            o_s2=vector,
        ),
        dict(
            s_pieces=pltpu.VMEM((2, pieces, AT_ALL // pieces + 16, features), BF),
            s_both=pltpu.VMEM((2 * V_ALL, features), F32),
            s_in=pltpu.VMEM((layers, features, 3 * features), F32),
            s_out=pltpu.VMEM((layers, features, features), F32),
            s_up=pltpu.VMEM((layers, features, 2 * features), F32),
            s_down=pltpu.VMEM((layers, 2 * features, features), F32),
            sems=pltpu.SemaphoreType.DMA((4 * layers,)),
        ),
        1 << 30,
        20,
    )
    return (layer_output, input_grad) + tuple(vars(result).values())


def solution(mesh):
    rows = P("dp", "pipe", None)
    return jax.shard_map(
        body,
        mesh=mesh,
        in_specs=(rows, P("dp", None), rows) + (P(),) * 12,
        out_specs=(rows, rows) + (P(),) * 12,
        check_vma=False,
    )
```

profile of v0, /device:TPU:0, one launch (start us, length us, event | category | flops | bytes accessed | tf_op | source)
XLA Modules:
  0.0 131.9 jit_solution(13128981745282995453)
XLA Ops:
  2.5 5.9 %collective-permute-start.2 = (bf16[2,320,256]{2,1,0:T(8,128)(2,1)S(1)}, bf16[2,320,256]{2,1,0:T(8,128)(2,1)S(1)}, u32[]{:S(2)}, u32[]{:S(2)}) collective-permute-start(bf16[2,320,256]{2,1,0:T(8,128)(2,1)S(1)} %get-tuple-element.99), channel_id=1, source_target_pairs={{0,1},{1,0},{2,3},{3,2},{4,5},{5,4},{6,7},{7,6},{8,9},{9,8},{10,11... | collective-permute-start | bytes 983048 | tf_op jit(solution)/shard_map/ppermute | solution.py:834
  9.1 2.0 %shard_map.254.refs_0_ = s32[72]{0:T(128)S(1)} custom-call(s32[2,2048]{1,0:T(2,128)S(1)} %copy-done, s32[1]{0:T(128)} %bitcast.refs_1_), custom_call_target="tpu_custom_call" | custom-call | flops 1048576 | bytes 8388608 | tf_op jit(solution)/shard_map/pallas_call | solution.py:718
  13.2 3.8 %collective-permute-done.2.refs_3_ = bf16[2,320,256]{2,1,0:T(8,128)(2,1)S(1)} collective-permute-done((bf16[2,320,256]{2,1,0:T(8,128)(2,1)S(1)}, bf16[2,320,256]{2,1,0:T(8,128)(2,1)S(1)}, u32[]{:S(2)}, u32[]{:S(2)}) %collective-permute-start.2) | collective-permute-done | bytes 327712 | tf_op jit(solution)/shard_map/ppermute | solution.py:834
  17.7 15.3 %shard_map.255 = (bf16[2816,256]{1,0:T(8,128)(2,1)}, bf16[2816,768]{1,0:T(8,128)(2,1)}, bf16[2816,256]{1,0:T(8,128)(2,1)}, bf16[2816,256]{1,0:T(8,128)(2,1)}, f3...) custom-call(s32[72]{0:T(128)} %copy-done.1, ...), custom_call_target="tpu_custom_call" | custom-call | flops 12884901888 | bytes 8388608 | tf_op jit(solution)/shard_map/pallas_call | solution.py:718
  33.9 40.6 %shard_map.256 = (bf16[8,144,256]{2,1,0:T(8,128)(2,1)}, bf16[8,144,256]{2,1,0:T(8,128)(2,1)}, bf16[8,128,256]{2,1,0:T(8,128)(2,1)}, bf16[8,128,256]{2,1,0:T(8,12...) custom-call(s32[72]{0:T(128)} %copy-done.1, s32[1]{0:T(128)} %bitcast.refs_1_, ...), custom_call_target="tpu_custom_call" | custom-call | flops 64424509440 | bytes 8388608 | tf_op jit(solution)/shard_map/pallas_call | solution.py:718
  75.1 1.7 %collective-permute-done.6 = bf16[8,144,256]{2,1,0:T(8,128)(2,1)S(1)} collective-permute-done((bf16[8,144,256]{2,1,0:T(8,128)(2,1)}, bf16[8,144,256]{2,1,0:T(8,128)(2,1)S(1)}, u32[]{:S(2)}, u32[]{:S(2)}) %collective-permute-start.6) | collective-permute-done | bytes 589856 | tf_op jit(solution)/shard_map/ppermute | solution.py:863
  76.8 1.3 %add_convert_fusion.1 = (bf16[4,144,256]{2,1,0:T(8,128)(2,1)S(1)}, bf16[4,144,256]{2,1,0:T(8,128)(2,1)S(1)}) fusion(bf16[8,144,256]{2,1,0:T(8,128)(2,1)S(1)} %collective-permute-done.6, bf16[8,144,256]{2,1,0:T(8,128)(2,1)} %get-tuple-element.68), kind=kLoop, calls=%fused_computation.10 | loop fusion | flops 1179648 | bytes 1769472 | tf_op jit(solution)/shard_map/convert_element_type | solution.py:867
  79.4 4.1 %collective-permute-start.16 = (bf16[4,128,256]{2,1,0:T(8,128)(2,1)S(1)}, bf16[4,128,256]{2,1,0:T(8,128)(2,1)S(1)}, u32[]{:S(2)}, u32[]{:S(2)}) collective-permute-start(bf16[4,128,256]{2,1,0:T(8,128)(2,1)S(1)} %get-tuple-element.93), channel_id=1, source_target_pairs={{0,16},{4,20},{8,24},{12,28},{16,0},{20,4},{24,8},{28,12},{1,17},{... | collective-permute-start | bytes 786440 | tf_op jit(solution)/shard_map/ppermute | solution.py:863
  83.5 6.5 %shard_map.257 = (bf16[2,2,512,256]{3,2,1,0:T(8,128)(2,1)S(1)}, bf16[2,2,320,256]{3,2,1,0:T(8,128)(2,1)S(1)}, bf16[2,2,320,256]{3,2,1,0:T(8,128)(2,1)S(1)}) custom-call(s32[72]{0:T(128)S(1)} %copy-done.2, s32[1]{0:T(128)} %bitcast.refs_1_, bf16[2816,256]{1,0:T(8,128)(2,1)S(1)} %copy-done.4, bf16[2816,256]{1,0:T(8,128)(2,1)S(1)} %copy-done.5), custom_call_target="tpu_custom_call" | custom-call | flops 2147483648 | bytes 8388608 | tf_op jit(solution)/shard_map/pallas_call | solution.py:718
  90.3 1.3 collective-permute-start.17
  91.5 3.8 %collective-permute-done.8 = bf16[2,144,256]{2,1,0:T(8,128)(2,1)S(1)} collective-permute-done((bf16[2,144,256]{2,1,0:T(8,128)(2,1)S(1)}, bf16[2,144,256]{2,1,0:T(8,128)(2,1)S(1)}, u32[]{:S(2)}, u32[]{:S(2)}) %collective-permute-start.8) | collective-permute-done | bytes 147488 | tf_op jit(solution)/shard_map/ppermute | solution.py:863
  95.5 2.1 %collective-permute-start.18 = (bf16[1,128,256]{2,1,0:T(8,128)(2,1)S(1)}, bf16[1,128,256]{2,1,0:T(8,128)(2,1)S(1)}, u32[]{:S(2)}, u32[]{:S(2)}) collective-permute-start(bf16[1,128,256]{2,1,0:T(8,128)(2,1)S(1)} %add_convert_fusion.14), channel_id=1, source_target_pairs={{0,1},{1,0},{2,3},{3,2},{4,5},{5,4},{6,7},{7,6},{8,9},{9,8},{10,11... | collective-permute-start | bytes 196616 | tf_op jit(solution)/shard_map/ppermute | solution.py:863
  97.5 2.9 %collective-permute-done.9 = bf16[1,144,256]{2,1,0:T(8,128)(2,1)S(1)} collective-permute-done((bf16[1,144,256]{2,1,0:T(8,128)(2,1)S(1)}, bf16[1,144,256]{2,1,0:T(8,128)(2,1)S(1)}, u32[]{:S(2)}, u32[]{:S(2)}) %collective-permute-start.9) | collective-permute-done | bytes 73760 | tf_op jit(solution)/shard_map/ppermute | solution.py:863
  101.3 2.2 %collective-permute-start.19 = (bf16[1,128,256]{2,1,0:T(8,128)(2,1)S(1)}, bf16[1,128,256]{2,1,0:T(8,128)(2,1)S(1)}, u32[]{:S(2)}, u32[]{:S(2)}) collective-permute-start(bf16[1,128,256]{2,1,0:T(8,128)(2,1)S(1)} %add_convert_fusion.13), channel_id=1, source_target_pairs={{0,2},{1,3},{2,0},{3,1},{4,6},{5,7},{6,4},{7,5},{8,10},{9,11},{10,... | collective-permute-start | bytes 196616 | tf_op jit(solution)/shard_map/ppermute | solution.py:863
  103.5 2.3 %collective-permute-done.10 = bf16[1,144,256]{2,1,0:T(8,128)(2,1)S(1)} collective-permute-done((bf16[1,144,256]{2,1,0:T(8,128)(2,1)S(1)}, bf16[1,144,256]{2,1,0:T(8,128)(2,1)S(1)}, u32[]{:S(2)}, u32[]{:S(2)}) %collective-permute-start.10) | collective-permute-done | bytes 73760 | tf_op jit(solution)/shard_map/ppermute | solution.py:863
  105.9 1.3 %collective-permute-done.19 = bf16[1,128,256]{2,1,0:T(8,128)(2,1)S(1)} collective-permute-done((bf16[1,128,256]{2,1,0:T(8,128)(2,1)S(1)}, bf16[1,128,256]{2,1,0:T(8,128)(2,1)S(1)}, u32[]{:S(2)}, u32[]{:S(2)}) %collective-permute-start.19) | collective-permute-done | bytes 65568 | tf_op jit(solution)/shard_map/ppermute | solution.py:863
  108.0 2.5 %collective-permute-done.11 = bf16[1,144,256]{2,1,0:T(8,128)(2,1)S(1)} collective-permute-done((bf16[1,144,256]{2,1,0:T(8,128)(2,1)S(1)}, bf16[1,144,256]{2,1,0:T(8,128)(2,1)S(1)}, u32[]{:S(2)}, u32[]{:S(2)}) %collective-permute-start.11) | collective-permute-done | bytes 73760 | tf_op jit(solution)/shard_map/ppermute | solution.py:863
  111.4 3.4 %collective-permute-start.4 = (bf16[2,2,320,256]{3,2,1,0:T(8,128)(2,1)S(1)}, bf16[2,2,320,256]{3,2,1,0:T(8,128)(2,1)S(1)}, u32[]{:S(2)}, u32[]{:S(2)}) collective-permute-start(bf16[2,2,320,256]{3,2,1,0:T(8,128)(2,1)S(1)} %get-tuple-element.89), channel_id=1, source_target_pairs={{0,1},{1,0},{2,3},{3,2},{4,5},{5,4},{6,7},{7,6},{8,9},{9,8},{10,11... | collective-permute-start | bytes 1966088 | tf_op jit(solution)/shard_map/ppermute | solution.py:834
  114.8 1.4 %collective-permute-start.21 = (bf16[2,128,256]{2,1,0:T(8,128)(2,1)S(1)}, bf16[2,128,256]{2,1,0:T(8,128)(2,1)S(1)}, u32[]{:S(2)}, u32[]{:S(2)}) collective-permute-start(bf16[2,128,256]{2,1,0:T(8,128)(2,1)S(1)} %pad_maximum_fusion.5), channel_id=1, source_target_pairs={{0,8},{4,12},{8,0},{12,4},{16,24},{20,28},{24,16},{28,20},{1,9},{5... | collective-permute-start | bytes 393224 | tf_op jit(solution)/shard_map/ppermute | solution.py:863
  117.0 2.8 %collective-permute-done.21 = bf16[2,128,256]{2,1,0:T(8,128)(2,1)S(1)} collective-permute-done((bf16[2,128,256]{2,1,0:T(8,128)(2,1)S(1)}, bf16[2,128,256]{2,1,0:T(8,128)(2,1)S(1)}, u32[]{:S(2)}, u32[]{:S(2)}) %collective-permute-start.21) | collective-permute-done | bytes 131104 | tf_op jit(solution)/shard_map/ppermute | solution.py:863
  120.9 2.1 %collective-permute-done.13 = bf16[4,144,256]{2,1,0:T(8,128)(2,1)S(1)} collective-permute-done((bf16[4,144,256]{2,1,0:T(8,128)(2,1)S(1)}, bf16[4,144,256]{2,1,0:T(8,128)(2,1)S(1)}, u32[]{:S(2)}, u32[]{:S(2)}) %collective-permute-start.13) | collective-permute-done | bytes 294944 | tf_op jit(solution)/shard_map/ppermute | solution.py:863
  123.2 3.1 %collective-permute-done.22 = bf16[4,128,256]{2,1,0:T(8,128)(2,1)S(1)} collective-permute-done((bf16[4,128,256]{2,1,0:T(8,128)(2,1)S(1)}, bf16[4,128,256]{2,1,0:T(8,128)(2,1)S(1)}, u32[]{:S(2)}, u32[]{:S(2)}) %collective-permute-start.22) | collective-permute-done | bytes 262176 | tf_op jit(solution)/shard_map/ppermute | solution.py:863
  126.6 1.3 fusion.5
  128.3 3.4 %shard_map.258 = (f32[2,256,768]{2,1,0:T(8,128)}, f32[2,512]{1,0:T(2,128)}, f32[2,256,256]{2,1,0:T(8,128)}, f32[2,256]{1,0:T(2,128)}, f32[2,256]{1,0:T(2,128)}, ...) custom-call(s32[2]{0:T(128)S(1)} %copy-done.3, ...), custom_call_target="tpu_custom_call" | custom-call | flops 1073741824 | bytes 8388608 | tf_op jit(solution)/shard_map/pallas_call | solution.py:718
  (73 shorter events, 13.6 us)
Async XLA Ops:
  1.8 11.3 %collective-permute-start.3 = (bf16[2,320,256]{2,1,0:T(8,128)(2,1)S(1)}, bf16[2,320,256]{2,1,0:T(8,128)(2,1)S(1)}, u32[]{:S(2)}, u32[]{:S(2)}) collective-permute-start(bf16[2,320,256]{2,1,0:T(8,128)(2,1)S(1)} %get-tuple-element.98), channel_id=1, source_target_pairs={{1,2},{2,1},{5,6},{6,5},{9,10},{10,9},{13,14},{14,13},{17,18},{18,... | collective-permute-start | bytes 983048 | tf_op jit(solution)/shard_map/ppermute | solution.py:834
  2.5 14.5 %collective-permute-start.2 = (bf16[2,320,256]{2,1,0:T(8,128)(2,1)S(1)}, bf16[2,320,256]{2,1,0:T(8,128)(2,1)S(1)}, u32[]{:S(2)}, u32[]{:S(2)}) collective-permute-start(bf16[2,320,256]{2,1,0:T(8,128)(2,1)S(1)} %get-tuple-element.99), channel_id=1, source_target_pairs={{0,1},{1,0},{2,3},{3,2},{4,5},{5,4},{6,7},{7,6},{8,9},{9,8},{10,11... | collective-permute-start | bytes 983048 | tf_op jit(solution)/shard_map/ppermute | solution.py:834
  11.8 21.3 %collective-permute-start = (bf16[2,320,256]{2,1,0:T(8,128)(2,1)S(1)}, bf16[2,320,256]{2,1,0:T(8,128)(2,1)S(1)}, u32[]{:S(2)}, u32[]{:S(2)}) collective-permute-start(bf16[2,320,256]{2,1,0:T(8,128)(2,1)S(1)} %get-tuple-element.49), channel_id=1, source_target_pairs={{0,1},{1,0},{2,3},{3,2},{4,5},{5,4},{6,7},{7,6},{8,9},{9,8},{10,11... | collective-permute-start | bytes 983048 | tf_op jit(solution)/shard_map/ppermute | solution.py:834
  11.8 21.2 %collective-permute-start.1 = (bf16[2,320,256]{2,1,0:T(8,128)(2,1)S(1)}, bf16[2,320,256]{2,1,0:T(8,128)(2,1)S(1)}, u32[]{:S(2)}, u32[]{:S(2)}) collective-permute-start(bf16[2,320,256]{2,1,0:T(8,128)(2,1)S(1)} %get-tuple-element.50), channel_id=1, source_target_pairs={{1,2},{2,1},{5,6},{6,5},{9,10},{10,9},{13,14},{14,13},{17,18},{18,... | collective-permute-start | bytes 983048 | tf_op jit(solution)/shard_map/ppermute | solution.py:834
  74.5 2.3 %collective-permute-start.6 = (bf16[8,144,256]{2,1,0:T(8,128)(2,1)}, bf16[8,144,256]{2,1,0:T(8,128)(2,1)S(1)}, u32[]{:S(2)}, u32[]{:S(2)}) collective-permute-start(bf16[8,144,256]{2,1,0:T(8,128)(2,1)} %get-tuple-element.69), channel_id=1, source_target_pairs={{0,4},{4,0},{8,12},{12,8},{16,20},{20,16},{24,28},{28,24},{1,5},{5... | collective-permute-start | bytes 1769480 | tf_op jit(solution)/shard_map/ppermute | solution.py:863
  74.6 3.6 %collective-permute-start.15 = (bf16[8,128,256]{2,1,0:T(8,128)(2,1)}, bf16[8,128,256]{2,1,0:T(8,128)(2,1)S(1)}, u32[]{:S(2)}, u32[]{:S(2)}) collective-permute-start(bf16[8,128,256]{2,1,0:T(8,128)(2,1)} %get-tuple-element.71), channel_id=1, source_target_pairs={{0,4},{4,0},{8,12},{12,8},{16,20},{20,16},{24,28},{28,24},{1,5},{5... | collective-permute-start | bytes 1572872 | tf_op jit(solution)/shard_map/ppermute | solution.py:863
  78.1 11.9 %collective-permute-start.7 = (bf16[4,144,256]{2,1,0:T(8,128)(2,1)S(1)}, bf16[4,144,256]{2,1,0:T(8,128)(2,1)S(1)}, u32[]{:S(2)}, u32[]{:S(2)}) collective-permute-start(bf16[4,144,256]{2,1,0:T(8,128)(2,1)S(1)} %get-tuple-element.91), channel_id=1, source_target_pairs={{0,8},{4,12},{8,0},{12,4},{16,24},{20,28},{24,16},{28,20},{1,9},{5... | collective-permute-start | bytes 884744 | tf_op jit(solution)/shard_map/ppermute | solution.py:863
  79.4 10.8 %collective-permute-start.16 = (bf16[4,128,256]{2,1,0:T(8,128)(2,1)S(1)}, bf16[4,128,256]{2,1,0:T(8,128)(2,1)S(1)}, u32[]{:S(2)}, u32[]{:S(2)}) collective-permute-start(bf16[4,128,256]{2,1,0:T(8,128)(2,1)S(1)} %get-tuple-element.93), channel_id=1, source_target_pairs={{0,16},{4,20},{8,24},{12,28},{16,0},{20,4},{24,8},{28,12},{1,17},{... | collective-permute-start | bytes 786440 | tf_op jit(solution)/shard_map/ppermute | solution.py:863
  90.1 5.2 %collective-permute-start.8 = (bf16[2,144,256]{2,1,0:T(8,128)(2,1)S(1)}, bf16[2,144,256]{2,1,0:T(8,128)(2,1)S(1)}, u32[]{:S(2)}, u32[]{:S(2)}) collective-permute-start(bf16[2,144,256]{2,1,0:T(8,128)(2,1)S(1)} %get-tuple-element.95), channel_id=1, source_target_pairs={{0,16},{4,20},{8,24},{12,28},{16,0},{20,4},{24,8},{28,12},{1,17},{... | collective-permute-start | bytes 442376 | tf_op jit(solution)/shard_map/ppermute | solution.py:863
  90.3 5.2 %collective-permute-start.17 = (bf16[2,128,256]{2,1,0:T(8,128)(2,1)S(1)}, bf16[2,128,256]{2,1,0:T(8,128)(2,1)S(1)}, u32[]{:S(2)}, u32[]{:S(2)}) collective-permute-start(bf16[2,128,256]{2,1,0:T(8,128)(2,1)S(1)} %get-tuple-element.97), channel_id=1, source_target_pairs={{0,8},{4,12},{8,0},{12,4},{16,24},{20,28},{24,16},{28,20},{1,9},{5... | collective-permute-start | bytes 393224 | tf_op jit(solution)/shard_map/ppermute | solution.py:863
  95.3 5.0 %collective-permute-start.9 = (bf16[1,144,256]{2,1,0:T(8,128)(2,1)S(1)}, bf16[1,144,256]{2,1,0:T(8,128)(2,1)S(1)}, u32[]{:S(2)}, u32[]{:S(2)}) collective-permute-start(bf16[1,144,256]{2,1,0:T(8,128)(2,1)S(1)} %add_convert_fusion.10), channel_id=1, source_target_pairs={{0,1},{1,0},{2,3},{3,2},{4,5},{5,4},{6,7},{7,6},{8,9},{9,8},{10,11... | collective-permute-start | bytes 221192 | tf_op jit(solution)/shard_map/ppermute | solution.py:863
  95.5 5.8 %collective-permute-start.18 = (bf16[1,128,256]{2,1,0:T(8,128)(2,1)S(1)}, bf16[1,128,256]{2,1,0:T(8,128)(2,1)S(1)}, u32[]{:S(2)}, u32[]{:S(2)}) collective-permute-start(bf16[1,128,256]{2,1,0:T(8,128)(2,1)S(1)} %add_convert_fusion.14), channel_id=1, source_target_pairs={{0,1},{1,0},{2,3},{3,2},{4,5},{5,4},{6,7},{7,6},{8,9},{9,8},{10,11... | collective-permute-start | bytes 196616 | tf_op jit(solution)/shard_map/ppermute | solution.py:863
  100.4 5.4 %collective-permute-start.10 = (bf16[1,144,256]{2,1,0:T(8,128)(2,1)S(1)}, bf16[1,144,256]{2,1,0:T(8,128)(2,1)S(1)}, u32[]{:S(2)}, u32[]{:S(2)}) collective-permute-start(bf16[1,144,256]{2,1,0:T(8,128)(2,1)S(1)} %add_convert_fusion.9), channel_id=1, source_target_pairs={{0,2},{1,3},{2,0},{3,1},{4,6},{5,7},{6,4},{7,5},{8,10},{9,11},{10,... | collective-permute-start | bytes 221192 | tf_op jit(solution)/shard_map/ppermute | solution.py:863
  101.3 5.9 %collective-permute-start.19 = (bf16[1,128,256]{2,1,0:T(8,128)(2,1)S(1)}, bf16[1,128,256]{2,1,0:T(8,128)(2,1)S(1)}, u32[]{:S(2)}, u32[]{:S(2)}) collective-permute-start(bf16[1,128,256]{2,1,0:T(8,128)(2,1)S(1)} %add_convert_fusion.13), channel_id=1, source_target_pairs={{0,2},{1,3},{2,0},{3,1},{4,6},{5,7},{6,4},{7,5},{8,10},{9,11},{10,... | collective-permute-start | bytes 196616 | tf_op jit(solution)/shard_map/ppermute | solution.py:863
  105.8 4.7 %collective-permute-start.11 = (bf16[1,144,256]{2,1,0:T(8,128)(2,1)S(1)}, bf16[1,144,256]{2,1,0:T(8,128)(2,1)S(1)}, u32[]{:S(2)}, u32[]{:S(2)}) collective-permute-start(bf16[1,144,256]{2,1,0:T(8,128)(2,1)S(1)} %add_convert_fusion.8), channel_id=1, source_target_pairs={{0,1},{1,0},{2,3},{3,2},{4,5},{5,4},{6,7},{7,6},{8,9},{9,8},{10,11... | collective-permute-start | bytes 221192 | tf_op jit(solution)/shard_map/ppermute | solution.py:863
  107.3 7.5 %collective-permute-start.20 = (bf16[1,128,256]{2,1,0:T(8,128)(2,1)S(1)}, bf16[1,128,256]{2,1,0:T(8,128)(2,1)S(1)}, u32[]{:S(2)}, u32[]{:S(2)}) collective-permute-start(bf16[1,128,256]{2,1,0:T(8,128)(2,1)S(1)} %add_convert_fusion.12), channel_id=1, source_target_pairs={{0,1},{1,0},{2,3},{3,2},{4,5},{5,4},{6,7},{7,6},{8,9},{9,8},{10,11... | collective-permute-start | bytes 196616 | tf_op jit(solution)/shard_map/ppermute | solution.py:863
  110.5 5.7 %collective-permute-start.12 = (bf16[2,144,256]{2,1,0:T(8,128)(2,1)S(1)}, bf16[2,144,256]{2,1,0:T(8,128)(2,1)S(1)}, u32[]{:S(2)}, u32[]{:S(2)}) collective-permute-start(bf16[2,144,256]{2,1,0:T(8,128)(2,1)S(1)} %pad_maximum_fusion.4), channel_id=1, source_target_pairs={{0,16},{4,20},{8,24},{12,28},{16,0},{20,4},{24,8},{28,12},{1,17},{... | collective-permute-start | bytes 442376 | tf_op jit(solution)/shard_map/ppermute | solution.py:863
  110.7 15.7 %collective-permute-start.5 = (bf16[2,2,320,256]{3,2,1,0:T(8,128)(2,1)S(1)}, bf16[2,2,320,256]{3,2,1,0:T(8,128)(2,1)S(1)}, u32[]{:S(2)}, u32[]{:S(2)}) collective-permute-start(bf16[2,2,320,256]{3,2,1,0:T(8,128)(2,1)S(1)} %get-tuple-element.88), channel_id=1, source_target_pairs={{1,2},{2,1},{5,6},{6,5},{9,10},{10,9},{13,14},{14,13},{17,18},{18,... | collective-permute-start | bytes 1966088 | tf_op jit(solution)/shard_map/ppermute | solution.py:834
  111.4 15.0 %collective-permute-start.4 = (bf16[2,2,320,256]{3,2,1,0:T(8,128)(2,1)S(1)}, bf16[2,2,320,256]{3,2,1,0:T(8,128)(2,1)S(1)}, u32[]{:S(2)}, u32[]{:S(2)}) collective-permute-start(bf16[2,2,320,256]{3,2,1,0:T(8,128)(2,1)S(1)} %get-tuple-element.89), channel_id=1, source_target_pairs={{0,1},{1,0},{2,3},{3,2},{4,5},{5,4},{6,7},{7,6},{8,9},{9,8},{10,11... | collective-permute-start | bytes 1966088 | tf_op jit(solution)/shard_map/ppermute | solution.py:834
  114.8 5.0 %collective-permute-start.21 = (bf16[2,128,256]{2,1,0:T(8,128)(2,1)S(1)}, bf16[2,128,256]{2,1,0:T(8,128)(2,1)S(1)}, u32[]{:S(2)}, u32[]{:S(2)}) collective-permute-start(bf16[2,128,256]{2,1,0:T(8,128)(2,1)S(1)} %pad_maximum_fusion.5), channel_id=1, source_target_pairs={{0,8},{4,12},{8,0},{12,4},{16,24},{20,28},{24,16},{28,20},{1,9},{5... | collective-permute-start | bytes 393224 | tf_op jit(solution)/shard_map/ppermute | solution.py:863
  116.2 6.8 %collective-permute-start.13 = (bf16[4,144,256]{2,1,0:T(8,128)(2,1)S(1)}, bf16[4,144,256]{2,1,0:T(8,128)(2,1)S(1)}, u32[]{:S(2)}, u32[]{:S(2)}) collective-permute-start(bf16[4,144,256]{2,1,0:T(8,128)(2,1)S(1)} %pad_maximum_fusion.2), channel_id=1, source_target_pairs={{0,8},{4,12},{8,0},{12,4},{16,24},{20,28},{24,16},{28,20},{1,9},{5... | collective-permute-start | bytes 884744 | tf_op jit(solution)/shard_map/ppermute | solution.py:863
  119.9 6.4 %collective-permute-start.22 = (bf16[4,128,256]{2,1,0:T(8,128)(2,1)S(1)}, bf16[4,128,256]{2,1,0:T(8,128)(2,1)S(1)}, u32[]{:S(2)}, u32[]{:S(2)}) collective-permute-start(bf16[4,128,256]{2,1,0:T(8,128)(2,1)S(1)} %pad_maximum_fusion.3), channel_id=1, source_target_pairs={{0,16},{4,20},{8,24},{12,28},{16,0},{20,4},{24,8},{28,12},{1,17},{... | collective-permute-start | bytes 786440 | tf_op jit(solution)/shard_map/ppermute | solution.py:863
  123.1 5.3 %collective-permute-start.14 = (bf16[8,144,256]{2,1,0:T(8,128)(2,1)S(1)}, bf16[8,144,256]{2,1,0:T(8,128)(2,1)S(1)}, u32[]{:S(2)}, u32[]{:S(2)}) collective-permute-start(bf16[8,144,256]{2,1,0:T(8,128)(2,1)S(1)} %pad_maximum_fusion.refs_1_), channel_id=1, source_target_pairs={{0,4},{4,0},{8,12},{12,8},{16,20},{20,16},{24,28},{28,24},{1,5},{5... | collective-permute-start | bytes 1769480 | tf_op jit(solution)/shard_map/ppermute | solution.py:863
  126.4 2.0 %collective-permute-start.23 = (bf16[8,128,256]{2,1,0:T(8,128)(2,1)S(1)}, bf16[8,128,256]{2,1,0:T(8,128)(2,1)S(1)}, u32[]{:S(2)}, u32[]{:S(2)}) collective-permute-start(bf16[8,128,256]{2,1,0:T(8,128)(2,1)S(1)} %pad_maximum_fusion.1.refs_3_), channel_id=1, source_target_pairs={{0,4},{4,0},{8,12},{12,8},{16,20},{20,16},{24,28},{28,24},{1,5},{5... | collective-permute-start | bytes 1572872 | tf_op jit(solution)/shard_map/ppermute | solution.py:863
  (11 other events, 40.3 us)
where the time goes:
time: 132 us
  Pallas kernels  67.8 us (51%)
  waiting for transfers between devices  27.1 us (21%)
  starting transfers between devices  26.7 us (20%)
  other arithmetic  6.3 us (5%)
  local copies, waits for them, and re-layouts  2.8 us (2%)
    pallas_call x5, Pallas kernels, call(): pl.pallas_call(run, out_shape=[jax.ShapeDtypeStruct(s, d) for s, d, _ in...  67.8 us
    ppermute x18, waiting for transfers between devices, exchange(): return lax.ppermute(value, axis, [(i, i ^ stride) for i in range(count)])  23.2 us
    ppermute x18, starting transfers between devices, exchange(): return lax.ppermute(value, axis, [(i, i ^ stride) for i in range(count)])  15.3 us
    ppermute x6, starting transfers between devices, halo(): lax.ppermute(value, 'pipe', [p for i, j in pairs for p in ((i, j), (j, i))])  11.4 us
    ppermute x6, waiting for transfers between devices, halo(): lax.ppermute(value, 'pipe', [p for i, j in pairs for p in ((i, j), (j, i))])  3.86 us
    unnamed x22, local copies, waits for them, and re-layouts  2.8 us
    convert_element_type x10, other arithmetic, added(): return (a.astype(F32) + b.astype(F32)).astype(BF)  2.8 us
  transfers between devices with their start and end apart: 24, of which 12 were waited for; matrix products, arithmetic and copies ran while one was open for 4% of the time, Pallas kernels for 18%

commit v1 on v0

--- a/solution.py
+++ b/solution.py
@@ -12,7 +12,8 @@
 MASKED = -1e30
 DOCS = 8
 REACH = 320
-TB = 512
+TB = 640
+TAIL = 256
 MOST_BLOCKS = 8
 QB = 128
 LANES = 128
@@ -21,20 +22,23 @@
 F32 = jnp.float32
 
 KEPT = dict(
-    x=(256, BF),
-    qkv=(768, BF),
-    ctx=(256, BF),
-    n1=(256, BF),
-    r1=(128, F32),
-    mid=(256, BF),
-    act=(512, BF),
-    slope=(512, BF),
-    n2=(256, BF),
-    r2=(128, F32),
+    ahead=(BF, dict(x=256, qkv=768)),
+    fed=(BF, dict(ctx=256, n1=256, mid=256, act=512, slope=512, n2=256)),
+    rates=(F32, dict(r1=128, r2=128)),
 )
 NAMES = tuple(KEPT)
 
 
+def kept_of(r):
+    found = {}
+    for name, (_, parts) in KEPT.items():
+        first = 0
+        for part, columns in parts.items():
+            found[part] = getattr(r, "s_" + name).at[:, first : first + columns]
+            first += columns
+    return SimpleNamespace(**found)
+
+
 def dot(a, b):
     return jnp.dot(a, b, preferred_element_type=F32)
 
@@ -57,6 +61,7 @@
 
 ITEMS = 2 * DOCS
 ROOM = ITEMS + 1
+SELF = 4 * ROOM + 4
 
 
 class Plan:
@@ -121,7 +126,7 @@
 
         @pl.when(self.odd == 1)
         def _():
-            visit(self.blocks, rows_at(self.blocks * TB, TB // 2))
+            visit(self.blocks, rows_at(self.blocks * TB, TAIL))
 
 
 def window_copies(win, span, own, low, high, sems, out):
@@ -158,20 +163,24 @@
 def pack(plan, most, win, dst):
     plan.over_blocks(lambda b, rows: clear(dst, rows))
 
-    def visit(d, n, length):
-        start, offset = plan.start(d), plan.offset(d)
-        shift = lax.bitwise_and(start, 15)
+    def visit(docs):
         row = lax.broadcasted_iota(jnp.int32, (QB, SPREAD), 0)
         col = lax.broadcasted_iota(jnp.int32, (QB, SPREAD), 1)
-        taken = col == row + shift
-        kept = jnp.where(taken & (row < length - (n - 1) * QB), 1.0, 0.0).astype(BF)
-        taken = jnp.where(taken, 1.0, 0.0).astype(BF)
-        rows = [win[rows_at(start - shift + q * QB, SPREAD), :] for q in range(n)]
-        picked = [dot(taken if q < n - 1 else kept, v).astype(BF) for q, v in enumerate(rows)]
-        for q, v in enumerate(picked):
-            dst[rows_at(offset + q * QB, QB), :] = v
-
-    plan.over_docs(most, visit)
+        parts = []
+        for d, n in docs:
+            start, length = plan.start(d), plan.length(d)
+            shift = lax.bitwise_and(start, 15)
+            whole = col == row + shift
+            for q in range(n):
+                inside = row < length - q * QB
+                taken = jnp.where(whole & inside if q == n - 1 or n == 2 else whole, 1.0, 0.0)
+                rows = win[rows_at(start - shift + q * QB, SPREAD), :]
+                parts.append((taken.astype(BF), rows, plan.offset(d) + q * QB))
+        picked = [dot(taken, rows).astype(BF) for taken, rows, _ in parts]
+        for v, (_, _, at) in zip(picked, parts):
+            dst[rows_at(at, QB), :] = v
+
+    plan.over_groups(most, visit)
 
 
 def unpack(plan, most, src, win, r, span, which):
@@ -215,7 +224,7 @@
 
 def turned_back(v):
     row = lax.broadcasted_iota(jnp.int32, (LANES, QB), 0)
-    return jnp.where(row < LANES // 2, v[:, :QB], v[:, QB:]).T
+    return jnp.where(row < LANES // 2, v[:, :QB], v[:, QB:]).astype(BF).T
 
 
 def turn(src, dst, first, width):
@@ -286,7 +295,7 @@
             share = jnp.where(column < length[i] - q * QB, 1.0 / total, 0.0)
             probs.append((raised * share).astype(BF))
         contexts = [dot(turned[i][g], v) for v, (i, _, g) in zip(probs, chains)]
-        contexts = [turned_back(v).astype(BF) for v in contexts]
+        contexts = [turned_back(v) for v in contexts]
         for v, context, (i, q, g) in zip(probs, contexts, chains):
             kept.ctx[rows_at(offset[i] + q * QB, QB), GROUPS[g]] = context
             n = docs[i][1]
@@ -441,7 +450,7 @@
             inner = jnp.sum(full * v, axis=0, keepdims=True)
             score_grads.append((full * (v - inner)).astype(BF))
         query_grads = [dot(turned[i][g], v) for v, (i, _, g) in zip(score_grads, chains)]
-        query_grads = [(turned_back(v) * scaling).astype(BF) for v in query_grads]
+        query_grads = [turned_back(v * scaling) for v in query_grads]
         sums = []
         for i in range(len(docs)):
             for g in range(2):
@@ -482,18 +491,18 @@
     plan.over_blocks(visit)
 
 
-def copies(r, kept, plan, out):
-    def one(name, rows, sem):
-        near = getattr(r if name == "probs" else kept, "s_probs" if name == "probs" else name)
-        far = getattr(r, ("o_" if out else "i_") + name)
-        ends = (near.at[rows], far.at[rows])
-        return pltpu.make_async_copy(*(ends if out else ends[::-1]), sem)
-
-    def of_block(names, b, rows):
-        return [one(k, rows, r.sems.at[NAMES.index(k), b]) for k in names]
+def copies(r, plan, out):
+    def one(near, far, sem):
+        return pltpu.make_async_copy(*((near, far) if out else (far, near)), sem)
+
+    def of_block(k, b, rows, first=0, columns=None):
+        near, far = (getattr(r, side + NAMES[k]) for side in ("s_", "o_" if out else "i_"))
+        at = (rows, slice(first, columns or near.shape[1]))
+        return [one(near.at[at], far.at[at], r.sems.at[k + (3 if columns else 0), b])]
 
     def of_doc(d, n):
-        return one("probs", pl.ds(plan.tile(d), max(n, 2) ** 2), r.sems.at[len(NAMES), 0])
+        at = pl.ds(plan.tile(d), max(n, 2) ** 2)
+        return one(r.s_probs.at[at], (r.o_probs if out else r.i_probs).at[at], r.sems.at[4, 0])
 
     return of_block, of_doc
 
@@ -516,26 +525,29 @@
     with_halos(r, r.s_window, span, started)
     w = layer_of(r, 0)
     plan = Plan(r)
-    kept = SimpleNamespace(**{k: getattr(r, "s_" + k) for k in NAMES})
-    of_block, of_doc = copies(r, kept, plan, True)
+    kept = kept_of(r)
+    of_block, of_doc = copies(r, plan, True)
     leaving = by_block(r.s_rows, r.o_next, r.out_sems)
     clear_between(r.s_window, span, r.own.shape[0])
     with_halos(r, r.s_window, span, waited)
     pack(plan, most, r.s_window, kept.x)
     waited(w.coming)
     project(plan, kept, w)
-    early, late = NAMES[:2], NAMES[2:]
-    plan.over_blocks(lambda b, rows: started(of_block(early, b, rows)))
+    plan.over_blocks(lambda b, rows: started(of_block(0, b, rows)))
     attend(plan, most, kept, r.s_probs, r.s_turned)
     plan.over_docs(most, lambda d, n, length: of_doc(d, n).start())
-    feed(plan, kept, w, r.s_rows, lambda b, rows: started(leaving(b, rows) + of_block(late, b, rows)))
-    plan.over_blocks(lambda b, rows: waited(leaving(b, rows) + of_block(NAMES, b, rows)))
+
+    def late(b, rows):
+        return leaving(b, rows) + of_block(1, b, rows) + of_block(2, b, rows)
+
+    feed(plan, kept, w, r.s_rows, lambda b, rows: started(late(b, rows)))
+    plan.over_blocks(lambda b, rows: waited(late(b, rows) + of_block(0, b, rows)))
     plan.over_docs(most, lambda d, n, length: of_doc(d, n).wait())
 
 
 def second_kernel(most, span, r):
     plan = Plan(r)
-    kept = SimpleNamespace(**{k: getattr(r, "s_" + k) for k in NAMES})
+    kept = kept_of(r)
     coming = by_block(r.x, kept.x, r.in_sems)
     plan.over_blocks(lambda b, rows: started(coming(b, rows)))
     w = layer_of(r, 1)
@@ -550,8 +562,17 @@
     with_halos(r, r.s_window, span, waited)
     pack(plan, most, r.s_window, r.s_rows)
     plan.over_blocks(lambda b, rows: waited(leaving(b, rows)))
-    of_block, of_doc = copies(r, kept, plan, False)
-    fed, projected, given = NAMES[2:], NAMES[1:2], NAMES[:1]
+    of_block, of_doc = copies(r, plan, False)
+
+    def fed(b, rows):
+        return of_block(1, b, rows) + of_block(2, b, rows)
+
+    def projected(b, rows):
+        return of_block(0, b, rows, 256)
+
+    def given(b, rows):
+        return of_block(0, b, rows, 0, 256)
+
     waited(below.coming)
     leaving = by_block(r.s_rows, r.o_grad, r.out_sems)
 
@@ -561,11 +582,11 @@
         def at(which, act):
             pl.when(step == which)(act)
 
-        def come(names, act):
-            plan.over_blocks(lambda b, rows: act(of_block(names, b, rows)))
+        def come(found, act):
+            plan.over_blocks(lambda b, rows: act(found(b, rows)))
 
         def before(b, rows):
-            at(1, lambda: waited(of_block(fed, b, rows)))
+            at(1, lambda: waited(fed(b, rows)))
 
         def after(b, rows):
             at(1, lambda: started(leaving(b, rows)))
@@ -590,12 +611,12 @@
         project_back(plan, kept, w, r, r.s_rows, after)
         at(0, lambda: come(given, started))
         r.s_both[pl.ds(pl.multiple_of((1 - step) * V_ALL, V_ALL), V_ALL), :] = r.s_small[...].sum(1)
-        at(0, lambda: send_pieces(r, r.o_keep1, r.o_send1, r.self[1]))
-        at(1, lambda: send_pieces(r, r.o_keep0, r.o_send0, r.self[0]))
+        at(0, lambda: send_pieces(r, r.o_keep1, r.o_send1, r.table[SELF + 1]))
+        at(1, lambda: send_pieces(r, r.o_keep0, r.o_send0, r.table[SELF]))
         return 0
 
     lax.fori_loop(0, 2, one, 0)
-    send_small(r, r.o_keep0, r.o_send0, r.self[0])
+    send_small(r, r.o_keep0, r.o_send0, r.table[SELF])
     plan.over_blocks(lambda b, rows: waited(leaving(b, rows)))
 
 
@@ -676,7 +697,7 @@
     sent = []
     for layer, (keep, got) in enumerate(((r.keep0, r.got0), (r.keep1, r.got1))):
         for p in range(count):
-            piece = lax.bitwise_xor(jnp.int32(p), r.self[layer])
+            piece = lax.bitwise_xor(jnp.int32(p), r.table[SELF + layer])
             source = keep if p < half else got
             r.s_pieces[layer, piece, 0 : keep.shape[1], :] = source[p % half]
         for low, high, near, far in big:
@@ -727,7 +748,7 @@
     return SimpleNamespace(**dict(zip(outputs, got)))
 
 
-def plan_kernel(sections, whole, span, r):
+def plan_kernel(sections, whole, span, ways, r):
     base = DOCS + 1
     huge = jnp.int32(1 << 20)
     for row in range(2):
@@ -743,8 +764,8 @@
             r.spent[row * base + doc] = spent
             if doc < DOCS:
                 size = starts[doc + 1] - starts[doc]
-                spent = spent + size + 230
-                spent = spent + jnp.where(size > 2 * QB, 270, 0) + jnp.where(size > 3 * QB, 330, 0)
+                spent = spent + size + 180
+                spent = spent + jnp.where(size > 2 * QB, 160, 0) + jnp.where(size > 3 * QB, 190, 0)
         for section in range(1, sections):
             low, high = jnp.int32(0), jnp.int32(0)
             for doc in range(base):
@@ -797,28 +818,41 @@
         low = jnp.where(place == section, cuts[section], low)
         high = jnp.where(place == section, cuts[section + 1], high)
     low, high = (low // base, low % base), (high // base, high % base)
-    k, offset, tile = jnp.int32(0), jnp.int32(0), jnp.int32(0)
     table = r.table
-    for row in range(2):
-
-        def one(doc, carry):
-            k, offset, tile = carry
-            begin = r.start[row * base + doc]
-            length = r.start[row * base + doc + 1] - begin
-            table[k] = begin - place * whole + REACH + row * span
-            table[ROOM + k] = length
-            table[2 * ROOM + k] = offset
-            table[3 * ROOM + k] = tile
-            blocks = jnp.maximum(lax.shift_right_logical(length + (QB - 1), 7), 2)
-            return k + 1, offset + lax.bitwise_and(length + 15, -16), tile + blocks * blocks
-
-        k, offset, tile = lax.fori_loop(low[row], high[row], one, (k, offset, tile))
+    carry = (jnp.int32(0), jnp.int32(0), jnp.int32(0))
+    for kind in range(2, whole // QB + 1):
+        for row in range(2):
+
+            def one(doc, carry):
+                k, offset, tile = carry
+                begin = r.start[row * base + doc]
+                length = r.start[row * base + doc + 1] - begin
+                blocks = jnp.maximum(lax.shift_right_logical(length + (QB - 1), 7), 2)
+                table[k] = begin - place * whole + REACH + row * span
+                table[ROOM + k] = length
+                table[2 * ROOM + k] = offset
+                table[3 * ROOM + k] = tile
+                taken = (blocks == kind).astype(jnp.int32)
+                offset = offset + taken * lax.bitwise_and(length + 15, -16)
+                return k + taken, offset, tile + taken * blocks * blocks
+
+            carry = lax.fori_loop(low[row], high[row], one, carry)
+    k, offset, _ = carry
     table[ROOM + k] = 0
-    halves = lax.shift_right_logical(offset + (TB // 2 - 1), 8)
+    blocks = offset // TB
+    rest = offset - blocks * TB
+    blocks = blocks + (rest > TAIL).astype(jnp.int32)
+    odd = ((rest > 0) & (rest <= TAIL)).astype(jnp.int32)
     table[4 * ROOM] = k
-    table[4 * ROOM + 1] = lax.shift_right_logical(halves, 1)
-    table[4 * ROOM + 2] = lax.bitwise_and(halves, 1)
-    table[4 * ROOM + 3] = halves * (TB // 2)
+    table[4 * ROOM + 1] = blocks
+    table[4 * ROOM + 2] = odd
+    table[4 * ROOM + 3] = blocks * TB + odd * TAIL
+    for i, order in enumerate(ways):
+        own = jnp.int32(0)
+        for axis, stride in order[:SPLIT]:
+            index = r.place[0] if axis == "pipe" else r.group[0]
+            own = 2 * own + lax.bitwise_and(index // stride, 1)
+        table[4 * ROOM + 4 + i] = own
 
 
 def halo_sent(low_part, high_part, place):
@@ -849,13 +883,6 @@
 
 
 SPLIT = 4
-
-
-def self_index(order):
-    index = jnp.int32(0)
-    for axis, stride in order[:SPLIT]:
-        index = 2 * index + lax.rem(lax.div(lax.axis_index(axis), stride), 2)
-    return index.astype(jnp.int32)
 
 
 def exchange(value, axis, stride):
@@ -910,7 +937,7 @@
     span = whole + 2 * REACH + 2 * QB
     most = whole // QB
     cap = row_count * (whole + 2 * REACH) + ITEMS * 15
-    cap = (cap + TB // 2 - 1) // (TB // 2) * (TB // 2) + 2 * QB
+    cap = (cap + TB - 1) // TB * TB + 2 * QB
     tiles = row_count * 53
     vmem = pl.BlockSpec(memory_space=pltpu.VMEM)
     smem = pl.BlockSpec(memory_space=pltpu.SMEM)
@@ -940,17 +967,20 @@
         weight_sems=pltpu.SemaphoreType.DMA((4 * attention_in.shape[0],)),
     )
 
-    order0, order1 = orders()
-    selves = [self_index(order0), self_index(order1)]
+    ways = orders()
     pieces = 1 << SPLIT
     even, odd = halo(halo_sent(tokens[:, :REACH], tokens[:, whole - REACH :], place))
     token_rows = dict(own=(tokens, anywhere), even=(even, anywhere), odd=(odd, anywhere))
     choices = section_count * (DOCS + 1) ** 2
     planned = call(
         plan_kernel,
-        (section_count, whole, span),
-        dict(segments=(segments, vmem), place=(place.reshape(1), smem)),
-        dict(table=((4 * ROOM + 4,), jnp.int32, smem)),
+        (section_count, whole, span, ways),
+        dict(
+            segments=(segments, vmem),
+            place=(place.reshape(1), smem),
+            group=(lax.axis_index("dp").astype(jnp.int32).reshape(1), smem),
+        ),
+        dict(table=((4 * ROOM + 6,), jnp.int32, smem)),
         dict(
             start=pltpu.SMEM((2 * (DOCS + 1),), jnp.int32),
             spent=pltpu.SMEM((2 * (DOCS + 1),), jnp.int32),
@@ -966,7 +996,7 @@
     sent = halo_sent(cotangent[:, :REACH], cotangent[:, whole - REACH :], place)
     even, odd = halo(lax.optimization_barrier((*sent, planned.table))[:2])
     cotangent_rows = dict(own=(cotangent, anywhere), even=(even, anywhere), odd=(odd, anywhere))
-    kept_scratch = {"s_" + k: pltpu.VMEM((cap, c), t) for k, (c, t) in KEPT.items()}
+    kept_scratch = {"s_" + k: pltpu.VMEM((cap, sum(c.values())), t) for k, (t, c) in KEPT.items()}
     kept_scratch.update(weight_scratch)
     probs_shape = (tiles, 2, QB, 2 * QB)
     kept_scratch.update(
@@ -974,7 +1004,7 @@
         s_window=pltpu.VMEM((row_count * span, features), BF),
         s_turned=pltpu.VMEM((features, whole), BF),
     )
-    sems = dict(sems=pltpu.SemaphoreType.DMA((len(NAMES) + 1, MOST_BLOCKS)))
+    sems = dict(sems=pltpu.SemaphoreType.DMA((5, MOST_BLOCKS)))
     moved = dict(
         s_rows=pltpu.VMEM((cap, features), BF),
         window_sems=pltpu.SemaphoreType.DMA((3 * row_count,)),
@@ -992,7 +1022,7 @@
         return ((pieces // 2, AT_ALL // pieces + extra, features), BF, vmem)
 
     rows_out = ((cap, features), BF, hbm)
-    kept_out = {"o_" + k: ((cap, c), t, hbm) for k, (c, t) in KEPT.items()}
+    kept_out = {"o_" + k: ((cap, sum(c.values())), t, hbm) for k, (t, c) in KEPT.items()}
     kept_out.update(o_probs=(probs_shape, BF, hbm), o_next=rows_out)
     shape = (most, span)
 
@@ -1012,7 +1042,7 @@
         plan
         | cotangent_rows
         | kept_in
-        | dict(x=(first.o_next, hbm), self=(jnp.stack(selves), smem))
+        | dict(x=(first.o_next, hbm))
         | weights,
         dict(
             o_keep0=pieces_out(16),
@@ -1031,10 +1061,10 @@
             s_spread=pltpu.VMEM((pieces, 16, features), F32),
         ),
         60 << 30,
-        57,
+        60,
     )
-    sums = [sum_steps(second.o_keep0, second.o_send0, order0)]
-    sums.append(sum_steps(second.o_keep1, second.o_send1, order1))
+    sums = [sum_steps(second.o_keep0, second.o_send0, ways[0])]
+    sums.append(sum_steps(second.o_keep1, second.o_send1, ways[1]))
     third = call(
         third_kernel,
         shape,
@@ -1074,7 +1104,7 @@
         last_kernel,
         (),
         dict(
-            self=(jnp.stack(selves), smem),
+            table=(planned.table, smem),
             keep0=(ends[0][0], vmem),
             got0=(ends[0][1], vmem),
             keep1=(ends[1][0], vmem),

time: 132 us -> 127 us (0.962)
  Pallas kernels: 67.8 us -> 61.7 us
  starting transfers between devices: 26.7 us -> 30 us
  waiting for transfers between devices: 27.1 us -> 24.5 us
    pallas_call x5, Pallas kernels: 67.8 us -> 61.7 us  [call(): pl.pallas_call(run, out_shape=[jax.ShapeDtypeStruct(s, d) for s, d, _ in...]
    ppermute x18, starting transfers between devices: 15.3 us -> 18.1 us  [exchange(): return lax.ppermute(value, axis, [(i, i ^ stride) for i in range(count)])]
    ppermute x18, waiting for transfers between devices: 23.2 us -> 21.6 us  [exchange(): return lax.ppermute(value, axis, [(i, i ^ stride) for i in range(count)])]
    unnamed x22 -> x18, local copies, waits for them, and re-layouts: 2.8 us -> 2.79 us
  transfers between devices with their start and end apart: 24 -> 24, of which waited for: 12 -> 13; matrix products, arithmetic and copies ran while one was open for 4% -> 4% of each run, Pallas kernels for 18% -> 17%
where the time goes in v1:
time: 127 us
  Pallas kernels  61.7 us (49%)
  starting transfers between devices  30 us (24%)
  waiting for transfers between devices  24.5 us (19%)
  other arithmetic  6.59 us (5%)
  local copies, waits for them, and re-layouts  2.79 us (2%)
    pallas_call x5, Pallas kernels, call(): pl.pallas_call(run, out_shape=[jax.ShapeDtypeStruct(s, d) for s, d, _ in...  61.7 us
    ppermute x18, waiting for transfers between devices, exchange(): return lax.ppermute(value, axis, [(i, i ^ stride) for i in range(count)])  21.6 us
    ppermute x18, starting transfers between devices, exchange(): return lax.ppermute(value, axis, [(i, i ^ stride) for i in range(count)])  18.1 us
    ppermute x6, starting transfers between devices, halo(): lax.ppermute(value, 'pipe', [p for i, j in pairs for p in ((i, j), (j, i))])  11.9 us
    ppermute x6, waiting for transfers between devices, halo(): lax.ppermute(value, 'pipe', [p for i, j in pairs for p in ((i, j), (j, i))])  2.94 us
    unnamed x18, local copies, waits for them, and re-layouts  2.79 us
    convert_element_type x10, other arithmetic, added(): return (a.astype(F32) + b.astype(F32)).astype(BF)  2.66 us
  transfers between devices with their start and end apart: 24, of which 13 were waited for; matrix products, arithmetic and copies ran while one was open for 4% of the time, Pallas kernels for 17%

profile of v1, /device:TPU:0, one launch (start us, length us, event | category | flops | bytes accessed | tf_op | source)
XLA Modules:
  0.0 126.8 jit_solution(2406663380140552723)
XLA Ops:
  2.5 5.9 %collective-permute-start.2 = (bf16[2,320,256]{2,1,0:T(8,128)(2,1)S(1)}, bf16[2,320,256]{2,1,0:T(8,128)(2,1)S(1)}, u32[]{:S(2)}, u32[]{:S(2)}) collective-permute-start(bf16[2,320,256]{2,1,0:T(8,128)(2,1)S(1)} %get-tuple-element.85), channel_id=1, source_target_pairs={{0,1},{1,0},{2,3},{3,2},{4,5},{5,4},{6,7},{7,6},{8,9},{9,8},{10,11... | collective-permute-start | bytes 983048 | tf_op jit(solution)/shard_map/ppermute | solution.py:868
  9.1 2.1 %shard_map.254.refs_0_ = s32[74]{0:T(128)S(1)} custom-call(s32[2,2048]{1,0:T(2,128)S(1)} %copy-done, s32[1]{0:T(128)} %bitcast.refs_1_, s32[1]{0:T(128)} %bitcast.1.refs_2_), custom_call_target="tpu_custom_call" | custom-call | flops 1048576 | bytes 8388608 | tf_op jit(solution)/shard_map/pallas_call | solution.py:739
  13.6 2.9 %collective-permute-done.2.refs_3_ = bf16[2,320,256]{2,1,0:T(8,128)(2,1)S(1)} collective-permute-done((bf16[2,320,256]{2,1,0:T(8,128)(2,1)S(1)}, bf16[2,320,256]{2,1,0:T(8,128)(2,1)S(1)}, u32[]{:S(2)}, u32[]{:S(2)}) %collective-permute-start.2) | collective-permute-done | bytes 327712 | tf_op jit(solution)/shard_map/ppermute | solution.py:868
  17.2 13.7 %shard_map.255 = (bf16[2816,1024]{1,0:T(8,128)(2,1)}, bf16[2816,2048]{1,0:T(8,128)(2,1)}, f32[2816,256]{1,0:T(8,128)}, bf16[106,2,128,256]{3,2,1,0:T(8,128)(2,1)}, bf16[2816,256]{1,0:T(8,128)(2,1)}) custom-call(s32[74]{0:T(128)} %copy-done.1, s32[1]{0:T(128)} %bitcast.refs_1_, bf16[2,512,256]{2,1,0:T(8,128)(2,1)} %refs_2_.2, bf16[2,320,256]{2,1,0:T(8,128)(2,1)} %copy-done.6, ...), custom_call_target="tpu_custom_call" | custom-call | flops 12884901888 | bytes 8388608 | tf_op jit(solution)/shard_map/pallas_call | solution.py:739
  31.8 36.9 %shard_map.256 = (bf16[8,144,256]{2,1,0:T(8,128)(2,1)}, bf16[8,144,256]{2,1,0:T(8,128)(2,1)}, bf16[8,128,256]{2,1,0:T(8,128)(2,1)}, bf16[8,128,256]{2,1,0:T(8,12...) custom-call(s32[74]{0:T(128)} %copy-done.1, s32[1]{0:T(128)} %bitcast.refs_1_, ...), custom_call_target="tpu_custom_call" | custom-call | flops 64424509440 | bytes 8388608 | tf_op jit(solution)/shard_map/pallas_call | solution.py:739
  69.3 1.7 %collective-permute-done.6 = bf16[8,144,256]{2,1,0:T(8,128)(2,1)S(1)} collective-permute-done((bf16[8,144,256]{2,1,0:T(8,128)(2,1)}, bf16[8,144,256]{2,1,0:T(8,128)(2,1)S(1)}, u32[]{:S(2)}, u32[]{:S(2)}) %collective-permute-start.6) | collective-permute-done | bytes 589856 | tf_op jit(solution)/shard_map/ppermute | solution.py:890
  73.5 4.5 %collective-permute-start.16 = (bf16[4,128,256]{2,1,0:T(8,128)(2,1)S(1)}, bf16[4,128,256]{2,1,0:T(8,128)(2,1)S(1)}, u32[]{:S(2)}, u32[]{:S(2)}) collective-permute-start(bf16[4,128,256]{2,1,0:T(8,128)(2,1)S(1)} %get-tuple-element.79), channel_id=1, source_target_pairs={{0,16},{4,20},{8,24},{12,28},{16,0},{20,4},{24,8},{28,12},{1,17},{... | collective-permute-start | bytes 786440 | tf_op jit(solution)/shard_map/ppermute | solution.py:890
  78.0 5.7 %shard_map.257 = (bf16[2,2,512,256]{3,2,1,0:T(8,128)(2,1)S(1)}, bf16[2,2,320,256]{3,2,1,0:T(8,128)(2,1)S(1)}, bf16[2,2,320,256]{3,2,1,0:T(8,128)(2,1)S(1)}) custom-call(s32[74]{0:T(128)S(1)} %copy-done.2, s32[1]{0:T(128)} %bitcast.refs_1_, bf16[2816,256]{1,0:T(8,128)(2,1)S(1)} %copy-done.3, bf16[2816,256]{1,0:T(8,128)(2,1)S(1)} %copy-done.4), custom_call_target="tpu_custom_call" | custom-call | flops 2147483648 | bytes 8388608 | tf_op jit(solution)/shard_map/pallas_call | solution.py:739
  84.4 1.7 %collective-permute-start.17 = (bf16[2,128,256]{2,1,0:T(8,128)(2,1)S(1)}, bf16[2,128,256]{2,1,0:T(8,128)(2,1)S(1)}, u32[]{:S(2)}, u32[]{:S(2)}) collective-permute-start(bf16[2,128,256]{2,1,0:T(8,128)(2,1)S(1)} %get-tuple-element.83), channel_id=1, source_target_pairs={{0,8},{4,12},{8,0},{12,4},{16,24},{20,28},{24,16},{28,20},{1,9},{5... | collective-permute-start | bytes 393224 | tf_op jit(solution)/shard_map/ppermute | solution.py:890
  86.1 2.9 %collective-permute-done.8 = bf16[2,144,256]{2,1,0:T(8,128)(2,1)S(1)} collective-permute-done((bf16[2,144,256]{2,1,0:T(8,128)(2,1)S(1)}, bf16[2,144,256]{2,1,0:T(8,128)(2,1)S(1)}, u32[]{:S(2)}, u32[]{:S(2)}) %collective-permute-start.8) | collective-permute-done | bytes 147488 | tf_op jit(solution)/shard_map/ppermute | solution.py:890
  89.0 3.0 %collective-permute-start.9 = (bf16[1,144,256]{2,1,0:T(8,128)(2,1)S(1)}, bf16[1,144,256]{2,1,0:T(8,128)(2,1)S(1)}, u32[]{:S(2)}, u32[]{:S(2)}) collective-permute-start(bf16[1,144,256]{2,1,0:T(8,128)(2,1)S(1)} %add_convert_fusion.10), channel_id=1, source_target_pairs={{0,1},{1,0},{2,3},{3,2},{4,5},{5,4},{6,7},{7,6},{8,9},{9,8},{10,11... | collective-permute-start | bytes 221192 | tf_op jit(solution)/shard_map/ppermute | solution.py:890
  92.2 2.4 %collective-permute-done.9 = bf16[1,144,256]{2,1,0:T(8,128)(2,1)S(1)} collective-permute-done((bf16[1,144,256]{2,1,0:T(8,128)(2,1)S(1)}, bf16[1,144,256]{2,1,0:T(8,128)(2,1)S(1)}, u32[]{:S(2)}, u32[]{:S(2)}) %collective-permute-start.9) | collective-permute-done | bytes 73760 | tf_op jit(solution)/shard_map/ppermute | solution.py:890
  95.4 1.8 %collective-permute-done.18 = bf16[1,128,256]{2,1,0:T(8,128)(2,1)S(1)} collective-permute-done((bf16[1,128,256]{2,1,0:T(8,128)(2,1)S(1)}, bf16[1,128,256]{2,1,0:T(8,128)(2,1)S(1)}, u32[]{:S(2)}, u32[]{:S(2)}) %collective-permute-start.18) | collective-permute-done | bytes 65568 | tf_op jit(solution)/shard_map/ppermute | solution.py:890
  97.8 2.3 %collective-permute-done.10 = bf16[1,144,256]{2,1,0:T(8,128)(2,1)S(1)} collective-permute-done((bf16[1,144,256]{2,1,0:T(8,128)(2,1)S(1)}, bf16[1,144,256]{2,1,0:T(8,128)(2,1)S(1)}, u32[]{:S(2)}, u32[]{:S(2)}) %collective-permute-start.10) | collective-permute-done | bytes 73760 | tf_op jit(solution)/shard_map/ppermute | solution.py:890
  100.1 2.4 %collective-permute-start.11 = (bf16[1,144,256]{2,1,0:T(8,128)(2,1)S(1)}, bf16[1,144,256]{2,1,0:T(8,128)(2,1)S(1)}, u32[]{:S(2)}, u32[]{:S(2)}) collective-permute-start(bf16[1,144,256]{2,1,0:T(8,128)(2,1)S(1)} %add_convert_fusion.8), channel_id=1, source_target_pairs={{0,1},{1,0},{2,3},{3,2},{4,5},{5,4},{6,7},{7,6},{8,9},{9,8},{10,11... | collective-permute-start | bytes 221192 | tf_op jit(solution)/shard_map/ppermute | solution.py:890
  103.4 1.5 %collective-permute-done.11 = bf16[1,144,256]{2,1,0:T(8,128)(2,1)S(1)} collective-permute-done((bf16[1,144,256]{2,1,0:T(8,128)(2,1)S(1)}, bf16[1,144,256]{2,1,0:T(8,128)(2,1)S(1)}, u32[]{:S(2)}, u32[]{:S(2)}) %collective-permute-start.11) | collective-permute-done | bytes 73760 | tf_op jit(solution)/shard_map/ppermute | solution.py:890
  105.8 3.8 %collective-permute-start.4 = (bf16[2,2,320,256]{3,2,1,0:T(8,128)(2,1)S(1)}, bf16[2,2,320,256]{3,2,1,0:T(8,128)(2,1)S(1)}, u32[]{:S(2)}, u32[]{:S(2)}) collective-permute-start(bf16[2,2,320,256]{3,2,1,0:T(8,128)(2,1)S(1)} %get-tuple-element.75), channel_id=1, source_target_pairs={{0,1},{1,0},{2,3},{3,2},{4,5},{5,4},{6,7},{7,6},{8,9},{9,8},{10,11... | collective-permute-start | bytes 1966088 | tf_op jit(solution)/shard_map/ppermute | solution.py:868
  109.7 1.7 %collective-permute-start.21 = (bf16[2,128,256]{2,1,0:T(8,128)(2,1)S(1)}, bf16[2,128,256]{2,1,0:T(8,128)(2,1)S(1)}, u32[]{:S(2)}, u32[]{:S(2)}) collective-permute-start(bf16[2,128,256]{2,1,0:T(8,128)(2,1)S(1)} %pad_maximum_fusion.5), channel_id=1, source_target_pairs={{0,8},{4,12},{8,0},{12,4},{16,24},{20,28},{24,16},{28,20},{1,9},{5... | collective-permute-start | bytes 393224 | tf_op jit(solution)/shard_map/ppermute | solution.py:890
  111.9 2.8 %collective-permute-done.21 = bf16[2,128,256]{2,1,0:T(8,128)(2,1)S(1)} collective-permute-done((bf16[2,128,256]{2,1,0:T(8,128)(2,1)S(1)}, bf16[2,128,256]{2,1,0:T(8,128)(2,1)S(1)}, u32[]{:S(2)}, u32[]{:S(2)}) %collective-permute-start.21) | collective-permute-done | bytes 131104 | tf_op jit(solution)/shard_map/ppermute | solution.py:890
  114.7 1.5 %collective-permute-start.22 = (bf16[4,128,256]{2,1,0:T(8,128)(2,1)S(1)}, bf16[4,128,256]{2,1,0:T(8,128)(2,1)S(1)}, u32[]{:S(2)}, u32[]{:S(2)}) collective-permute-start(bf16[4,128,256]{2,1,0:T(8,128)(2,1)S(1)} %pad_maximum_fusion.3), channel_id=1, source_target_pairs={{0,16},{4,20},{8,24},{12,28},{16,0},{20,4},{24,8},{28,12},{1,17},{... | collective-permute-start | bytes 786440 | tf_op jit(solution)/shard_map/ppermute | solution.py:890
  116.3 1.9 %collective-permute-done.13 = bf16[4,144,256]{2,1,0:T(8,128)(2,1)S(1)} collective-permute-done((bf16[4,144,256]{2,1,0:T(8,128)(2,1)S(1)}, bf16[4,144,256]{2,1,0:T(8,128)(2,1)S(1)}, u32[]{:S(2)}, u32[]{:S(2)}) %collective-permute-start.13) | collective-permute-done | bytes 294944 | tf_op jit(solution)/shard_map/ppermute | solution.py:890
  118.3 2.8 %collective-permute-done.22 = bf16[4,128,256]{2,1,0:T(8,128)(2,1)S(1)} collective-permute-done((bf16[4,128,256]{2,1,0:T(8,128)(2,1)S(1)}, bf16[4,128,256]{2,1,0:T(8,128)(2,1)S(1)}, u32[]{:S(2)}, u32[]{:S(2)}) %collective-permute-start.22) | collective-permute-done | bytes 262176 | tf_op jit(solution)/shard_map/ppermute | solution.py:890
  121.4 1.3 %fusion.5 = (bf16[2,512,256]{2,1,0:T(8,128)(2,1)}, bf16[2,512,256]{2,1,0:T(8,128)(2,1)}) fusion(bf16[2,2,320,256]{3,2,1,0:T(8,128)(2,1)S(1)} %get-tuple-element.73, bf16[2,2,320,256]{3,2,1,0:T(8,128)(2,1)S(1)} %get-tuple-element.72, bf16[2,2,512,256]{3,2,1,0:T(8,128)(2,1)S(1)} %get-tuple-element.51), kind=kLoop, calls=%fused_computation.16 | loop fusion | flops 3145728 | bytes 3407872 | tf_op jit(solution)/shard_map/add | solution.py:1091
  123.2 3.4 %shard_map.258 = (f32[2,256,768]{2,1,0:T(8,128)}, f32[2,512]{1,0:T(2,128)}, f32[2,256,256]{2,1,0:T(8,128)}, f32[2,256]{1,0:T(2,128)}, f32[2,256]{1,0:T(2,128)}, ...) custom-call(s32[74]{0:T(128)S(1)} %copy-done.2, ...), custom_call_target="tpu_custom_call" | custom-call | flops 1073741824 | bytes 8388608 | tf_op jit(solution)/shard_map/pallas_call | solution.py:739
  (68 shorter events, 14.9 us)
Async XLA Ops:
  1.8 11.8 %collective-permute-start.3 = (bf16[2,320,256]{2,1,0:T(8,128)(2,1)S(1)}, bf16[2,320,256]{2,1,0:T(8,128)(2,1)S(1)}, u32[]{:S(2)}, u32[]{:S(2)}) collective-permute-start(bf16[2,320,256]{2,1,0:T(8,128)(2,1)S(1)} %get-tuple-element.84), channel_id=1, source_target_pairs={{1,2},{2,1},{5,6},{6,5},{9,10},{10,9},{13,14},{14,13},{17,18},{18,... | collective-permute-start | bytes 983048 | tf_op jit(solution)/shard_map/ppermute | solution.py:868
  2.5 14.0 %collective-permute-start.2 = (bf16[2,320,256]{2,1,0:T(8,128)(2,1)S(1)}, bf16[2,320,256]{2,1,0:T(8,128)(2,1)S(1)}, u32[]{:S(2)}, u32[]{:S(2)}) collective-permute-start(bf16[2,320,256]{2,1,0:T(8,128)(2,1)S(1)} %get-tuple-element.85), channel_id=1, source_target_pairs={{0,1},{1,0},{2,3},{3,2},{4,5},{5,4},{6,7},{7,6},{8,9},{9,8},{10,11... | collective-permute-start | bytes 983048 | tf_op jit(solution)/shard_map/ppermute | solution.py:868
  12.8 18.1 %collective-permute-start = (bf16[2,320,256]{2,1,0:T(8,128)(2,1)S(1)}, bf16[2,320,256]{2,1,0:T(8,128)(2,1)S(1)}, u32[]{:S(2)}, u32[]{:S(2)}) collective-permute-start(bf16[2,320,256]{2,1,0:T(8,128)(2,1)S(1)} %get-tuple-element.42), channel_id=1, source_target_pairs={{0,1},{1,0},{2,3},{3,2},{4,5},{5,4},{6,7},{7,6},{8,9},{9,8},{10,11... | collective-permute-start | bytes 983048 | tf_op jit(solution)/shard_map/ppermute | solution.py:868
  12.9 18.1 %collective-permute-start.1 = (bf16[2,320,256]{2,1,0:T(8,128)(2,1)S(1)}, bf16[2,320,256]{2,1,0:T(8,128)(2,1)S(1)}, u32[]{:S(2)}, u32[]{:S(2)}) collective-permute-start(bf16[2,320,256]{2,1,0:T(8,128)(2,1)S(1)} %get-tuple-element.43), channel_id=1, source_target_pairs={{1,2},{2,1},{5,6},{6,5},{9,10},{10,9},{13,14},{14,13},{17,18},{18,... | collective-permute-start | bytes 983048 | tf_op jit(solution)/shard_map/ppermute | solution.py:868
  68.8 2.3 %collective-permute-start.6 = (bf16[8,144,256]{2,1,0:T(8,128)(2,1)}, bf16[8,144,256]{2,1,0:T(8,128)(2,1)S(1)}, u32[]{:S(2)}, u32[]{:S(2)}) collective-permute-start(bf16[8,144,256]{2,1,0:T(8,128)(2,1)} %get-tuple-element.55), channel_id=1, source_target_pairs={{0,4},{4,0},{8,12},{12,8},{16,20},{20,16},{24,28},{28,24},{1,5},{5... | collective-permute-start | bytes 1769480 | tf_op jit(solution)/shard_map/ppermute | solution.py:890
  68.8 3.5 %collective-permute-start.15 = (bf16[8,128,256]{2,1,0:T(8,128)(2,1)}, bf16[8,128,256]{2,1,0:T(8,128)(2,1)S(1)}, u32[]{:S(2)}, u32[]{:S(2)}) collective-permute-start(bf16[8,128,256]{2,1,0:T(8,128)(2,1)} %get-tuple-element.57), channel_id=1, source_target_pairs={{0,4},{4,0},{8,12},{12,8},{16,20},{20,16},{24,28},{28,24},{1,5},{5... | collective-permute-start | bytes 1572872 | tf_op jit(solution)/shard_map/ppermute | solution.py:890
  72.3 11.4 %collective-permute-start.7 = (bf16[4,144,256]{2,1,0:T(8,128)(2,1)S(1)}, bf16[4,144,256]{2,1,0:T(8,128)(2,1)S(1)}, u32[]{:S(2)}, u32[]{:S(2)}) collective-permute-start(bf16[4,144,256]{2,1,0:T(8,128)(2,1)S(1)} %get-tuple-element.77), channel_id=1, source_target_pairs={{0,8},{4,12},{8,0},{12,4},{16,24},{20,28},{24,16},{28,20},{1,9},{5... | collective-permute-start | bytes 884744 | tf_op jit(solution)/shard_map/ppermute | solution.py:890
  73.5 10.8 %collective-permute-start.16 = (bf16[4,128,256]{2,1,0:T(8,128)(2,1)S(1)}, bf16[4,128,256]{2,1,0:T(8,128)(2,1)S(1)}, u32[]{:S(2)}, u32[]{:S(2)}) collective-permute-start(bf16[4,128,256]{2,1,0:T(8,128)(2,1)S(1)} %get-tuple-element.79), channel_id=1, source_target_pairs={{0,16},{4,20},{8,24},{12,28},{16,0},{20,4},{24,8},{28,12},{1,17},{... | collective-permute-start | bytes 786440 | tf_op jit(solution)/shard_map/ppermute | solution.py:890
  83.8 5.2 %collective-permute-start.8 = (bf16[2,144,256]{2,1,0:T(8,128)(2,1)S(1)}, bf16[2,144,256]{2,1,0:T(8,128)(2,1)S(1)}, u32[]{:S(2)}, u32[]{:S(2)}) collective-permute-start(bf16[2,144,256]{2,1,0:T(8,128)(2,1)S(1)} %get-tuple-element.81), channel_id=1, source_target_pairs={{0,16},{4,20},{8,24},{12,28},{16,0},{20,4},{24,8},{28,12},{1,17},{... | collective-permute-start | bytes 442376 | tf_op jit(solution)/shard_map/ppermute | solution.py:890
  84.4 7.6 %collective-permute-start.17 = (bf16[2,128,256]{2,1,0:T(8,128)(2,1)S(1)}, bf16[2,128,256]{2,1,0:T(8,128)(2,1)S(1)}, u32[]{:S(2)}, u32[]{:S(2)}) collective-permute-start(bf16[2,128,256]{2,1,0:T(8,128)(2,1)S(1)} %get-tuple-element.83), channel_id=1, source_target_pairs={{0,8},{4,12},{8,0},{12,4},{16,24},{20,28},{24,16},{28,20},{1,9},{5... | collective-permute-start | bytes 393224 | tf_op jit(solution)/shard_map/ppermute | solution.py:890
  89.0 5.7 %collective-permute-start.9 = (bf16[1,144,256]{2,1,0:T(8,128)(2,1)S(1)}, bf16[1,144,256]{2,1,0:T(8,128)(2,1)S(1)}, u32[]{:S(2)}, u32[]{:S(2)}) collective-permute-start(bf16[1,144,256]{2,1,0:T(8,128)(2,1)S(1)} %add_convert_fusion.10), channel_id=1, source_target_pairs={{0,1},{1,0},{2,3},{3,2},{4,5},{5,4},{6,7},{7,6},{8,9},{9,8},{10,11... | collective-permute-start | bytes 221192 | tf_op jit(solution)/shard_map/ppermute | solution.py:890
  92.0 5.1 %collective-permute-start.18 = (bf16[1,128,256]{2,1,0:T(8,128)(2,1)S(1)}, bf16[1,128,256]{2,1,0:T(8,128)(2,1)S(1)}, u32[]{:S(2)}, u32[]{:S(2)}) collective-permute-start(bf16[1,128,256]{2,1,0:T(8,128)(2,1)S(1)} %add_convert_fusion.14), channel_id=1, source_target_pairs={{0,1},{1,0},{2,3},{3,2},{4,5},{5,4},{6,7},{7,6},{8,9},{9,8},{10,11... | collective-permute-start | bytes 196616 | tf_op jit(solution)/shard_map/ppermute | solution.py:890
  94.7 5.4 %collective-permute-start.10 = (bf16[1,144,256]{2,1,0:T(8,128)(2,1)S(1)}, bf16[1,144,256]{2,1,0:T(8,128)(2,1)S(1)}, u32[]{:S(2)}, u32[]{:S(2)}) collective-permute-start(bf16[1,144,256]{2,1,0:T(8,128)(2,1)S(1)} %add_convert_fusion.9), channel_id=1, source_target_pairs={{0,2},{1,3},{2,0},{3,1},{4,6},{5,7},{6,4},{7,5},{8,10},{9,11},{10,... | collective-permute-start | bytes 221192 | tf_op jit(solution)/shard_map/ppermute | solution.py:890
  97.2 6.1 %collective-permute-start.19 = (bf16[1,128,256]{2,1,0:T(8,128)(2,1)S(1)}, bf16[1,128,256]{2,1,0:T(8,128)(2,1)S(1)}, u32[]{:S(2)}, u32[]{:S(2)}) collective-permute-start(bf16[1,128,256]{2,1,0:T(8,128)(2,1)S(1)} %add_convert_fusion.13), channel_id=1, source_target_pairs={{0,2},{1,3},{2,0},{3,1},{4,6},{5,7},{6,4},{7,5},{8,10},{9,11},{10,... | collective-permute-start | bytes 196616 | tf_op jit(solution)/shard_map/ppermute | solution.py:890
  100.1 4.8 %collective-permute-start.11 = (bf16[1,144,256]{2,1,0:T(8,128)(2,1)S(1)}, bf16[1,144,256]{2,1,0:T(8,128)(2,1)S(1)}, u32[]{:S(2)}, u32[]{:S(2)}) collective-permute-start(bf16[1,144,256]{2,1,0:T(8,128)(2,1)S(1)} %add_convert_fusion.8), channel_id=1, source_target_pairs={{0,1},{1,0},{2,3},{3,2},{4,5},{5,4},{6,7},{7,6},{8,9},{9,8},{10,11... | collective-permute-start | bytes 221192 | tf_op jit(solution)/shard_map/ppermute | solution.py:890
  103.3 6.3 %collective-permute-start.20 = (bf16[1,128,256]{2,1,0:T(8,128)(2,1)S(1)}, bf16[1,128,256]{2,1,0:T(8,128)(2,1)S(1)}, u32[]{:S(2)}, u32[]{:S(2)}) collective-permute-start(bf16[1,128,256]{2,1,0:T(8,128)(2,1)S(1)} %add_convert_fusion.12), channel_id=1, source_target_pairs={{0,1},{1,0},{2,3},{3,2},{4,5},{5,4},{6,7},{7,6},{8,9},{9,8},{10,11... | collective-permute-start | bytes 196616 | tf_op jit(solution)/shard_map/ppermute | solution.py:890
  104.9 6.4 %collective-permute-start.12 = (bf16[2,144,256]{2,1,0:T(8,128)(2,1)S(1)}, bf16[2,144,256]{2,1,0:T(8,128)(2,1)S(1)}, u32[]{:S(2)}, u32[]{:S(2)}) collective-permute-start(bf16[2,144,256]{2,1,0:T(8,128)(2,1)S(1)} %pad_maximum_fusion.4), channel_id=1, source_target_pairs={{0,16},{4,20},{8,24},{12,28},{16,0},{20,4},{24,8},{28,12},{1,17},{... | collective-permute-start | bytes 442376 | tf_op jit(solution)/shard_map/ppermute | solution.py:890
  105.1 16.2 %collective-permute-start.5 = (bf16[2,2,320,256]{3,2,1,0:T(8,128)(2,1)S(1)}, bf16[2,2,320,256]{3,2,1,0:T(8,128)(2,1)S(1)}, u32[]{:S(2)}, u32[]{:S(2)}) collective-permute-start(bf16[2,2,320,256]{3,2,1,0:T(8,128)(2,1)S(1)} %get-tuple-element.74), channel_id=1, source_target_pairs={{1,2},{2,1},{5,6},{6,5},{9,10},{10,9},{13,14},{14,13},{17,18},{18,... | collective-permute-start | bytes 1966088 | tf_op jit(solution)/shard_map/ppermute | solution.py:868
  105.8 15.5 %collective-permute-start.4 = (bf16[2,2,320,256]{3,2,1,0:T(8,128)(2,1)S(1)}, bf16[2,2,320,256]{3,2,1,0:T(8,128)(2,1)S(1)}, u32[]{:S(2)}, u32[]{:S(2)}) collective-permute-start(bf16[2,2,320,256]{3,2,1,0:T(8,128)(2,1)S(1)} %get-tuple-element.75), channel_id=1, source_target_pairs={{0,1},{1,0},{2,3},{3,2},{4,5},{5,4},{6,7},{7,6},{8,9},{9,8},{10,11... | collective-permute-start | bytes 1966088 | tf_op jit(solution)/shard_map/ppermute | solution.py:868
  109.7 5.0 %collective-permute-start.21 = (bf16[2,128,256]{2,1,0:T(8,128)(2,1)S(1)}, bf16[2,128,256]{2,1,0:T(8,128)(2,1)S(1)}, u32[]{:S(2)}, u32[]{:S(2)}) collective-permute-start(bf16[2,128,256]{2,1,0:T(8,128)(2,1)S(1)} %pad_maximum_fusion.5), channel_id=1, source_target_pairs={{0,8},{4,12},{8,0},{12,4},{16,24},{20,28},{24,16},{28,20},{1,9},{5... | collective-permute-start | bytes 393224 | tf_op jit(solution)/shard_map/ppermute | solution.py:890
  111.4 6.8 %collective-permute-start.13 = (bf16[4,144,256]{2,1,0:T(8,128)(2,1)S(1)}, bf16[4,144,256]{2,1,0:T(8,128)(2,1)S(1)}, u32[]{:S(2)}, u32[]{:S(2)}) collective-permute-start(bf16[4,144,256]{2,1,0:T(8,128)(2,1)S(1)} %pad_maximum_fusion.2), channel_id=1, source_target_pairs={{0,8},{4,12},{8,0},{12,4},{16,24},{20,28},{24,16},{28,20},{1,9},{5... | collective-permute-start | bytes 884744 | tf_op jit(solution)/shard_map/ppermute | solution.py:890
  114.7 6.4 %collective-permute-start.22 = (bf16[4,128,256]{2,1,0:T(8,128)(2,1)S(1)}, bf16[4,128,256]{2,1,0:T(8,128)(2,1)S(1)}, u32[]{:S(2)}, u32[]{:S(2)}) collective-permute-start(bf16[4,128,256]{2,1,0:T(8,128)(2,1)S(1)} %pad_maximum_fusion.3), channel_id=1, source_target_pairs={{0,16},{4,20},{8,24},{12,28},{16,0},{20,4},{24,8},{28,12},{1,17},{... | collective-permute-start | bytes 786440 | tf_op jit(solution)/shard_map/ppermute | solution.py:890
  118.2 5.0 %collective-permute-start.14 = (bf16[8,144,256]{2,1,0:T(8,128)(2,1)S(1)}, bf16[8,144,256]{2,1,0:T(8,128)(2,1)S(1)}, u32[]{:S(2)}, u32[]{:S(2)}) collective-permute-start(bf16[8,144,256]{2,1,0:T(8,128)(2,1)S(1)} %pad_maximum_fusion.refs_1_), channel_id=1, source_target_pairs={{0,4},{4,0},{8,12},{12,8},{16,20},{20,16},{24,28},{28,24},{1,5},{5... | collective-permute-start | bytes 1769480 | tf_op jit(solution)/shard_map/ppermute | solution.py:890
  121.2 2.0 %collective-permute-start.23 = (bf16[8,128,256]{2,1,0:T(8,128)(2,1)S(1)}, bf16[8,128,256]{2,1,0:T(8,128)(2,1)S(1)}, u32[]{:S(2)}, u32[]{:S(2)}) collective-permute-start(bf16[8,128,256]{2,1,0:T(8,128)(2,1)S(1)} %pad_maximum_fusion.1.refs_3_), channel_id=1, source_target_pairs={{0,4},{4,0},{8,12},{12,8},{16,20},{20,16},{24,28},{28,24},{1,5},{5... | collective-permute-start | bytes 1572872 | tf_op jit(solution)/shard_map/ppermute | solution.py:890
  (9 other events, 34.1 us)

commit v2 on v1

--- a/solution.py
+++ b/solution.py
@@ -1033,7 +1033,7 @@
         kept_out,
         kept_scratch | sems | moved,
         12 << 30,
-        60,
+        63,
     )
     kept_in = {"i_" + k: (getattr(first, "o_" + k), hbm) for k in NAMES + ("probs",)}
     second = call(
@@ -1061,7 +1061,7 @@
             s_spread=pltpu.VMEM((pieces, 16, features), F32),
         ),
         60 << 30,
-        60,
+        63,
     )
     sums = [sum_steps(second.o_keep0, second.o_send0, ways[0])]
     sums.append(sum_steps(second.o_keep1, second.o_send1, ways[1]))

time: 127 us -> 127 us (level)
  local copies, waits for them, and re-layouts: 2.79 us -> 1.24 us
  waiting for transfers between devices: 24.5 us -> 23.2 us
  Pallas kernels: 61.7 us -> 63 us
    unnamed x18 -> x12, local copies, waits for them, and re-layouts: 2.79 us -> 1.24 us
    pallas_call x5, Pallas kernels: 61.7 us -> 63 us  [call(): pl.pallas_call(run, out_shape=[jax.ShapeDtypeStruct(s, d) for s, d, _ in...]
  transfers between devices with their start and end apart: 24 -> 24, of which waited for: 13 -> 14; matrix products, arithmetic and copies ran while one was open for 4% -> 4% of each run, Pallas kernels for 17% -> 17%
where the time goes in v2:
time: 127 us; the launch traced here: 126 us
  Pallas kernels  63 us (50%)
  starting transfers between devices  30.5 us (24%)
  waiting for transfers between devices  23.2 us (18%)
  other arithmetic  6.59 us (5%)
    pallas_call x5, Pallas kernels, call(): pl.pallas_call(run, out_shape=[jax.ShapeDtypeStruct(s, d) for s, d, _ in...  63 us
    ppermute x18, waiting for transfers between devices, exchange(): return lax.ppermute(value, axis, [(i, i ^ stride) for i in range(count)])  21.2 us
    ppermute x18, starting transfers between devices, exchange(): return lax.ppermute(value, axis, [(i, i ^ stride) for i in range(count)])  18.9 us
    ppermute x6, starting transfers between devices, halo(): lax.ppermute(value, 'pipe', [p for i, j in pairs for p in ((i, j), (j, i))])  11.7 us
    convert_element_type x10, other arithmetic, added(): return (a.astype(F32) + b.astype(F32)).astype(BF)  2.65 us
  transfers between devices with their start and end apart: 24, of which 14 were waited for; matrix products, arithmetic and copies ran while one was open for 4% of the time, Pallas kernels for 17%

profile of v2, /device:TPU:0, one launch (start us, length us, event | category | flops | bytes accessed | tf_op | source)
XLA Modules:
  0.0 125.7 jit_solution(10094722464005021341)
XLA Ops:
  2.5 5.9 %collective-permute-start.2 = (bf16[2,320,256]{2,1,0:T(8,128)(2,1)S(1)}, bf16[2,320,256]{2,1,0:T(8,128)(2,1)}, u32[]{:S(2)}, u32[]{:S(2)}) collective-permute-start(bf16[2,320,256]{2,1,0:T(8,128)(2,1)S(1)} %get-tuple-element.85), channel_id=1, source_target_pairs={{0,1},{1,0},{2,3},{3,2},{4,5},{5,4},{6,7},{7,6},{8,9},{9,8},{10,11... | collective-permute-start | bytes 983048 | tf_op jit(solution)/shard_map/ppermute | solution.py:868
  9.1 2.7 %shard_map.254.refs_0_ = s32[74]{0:T(128)S(1)} custom-call(s32[2,2048]{1,0:T(2,128)S(1)} %copy-done, s32[1]{0:T(128)} %bitcast.refs_1_, s32[1]{0:T(128)} %bitcast.1.refs_2_), custom_call_target="tpu_custom_call" | custom-call | flops 1048576 | bytes 8388608 | tf_op jit(solution)/shard_map/pallas_call | solution.py:739
  13.7 1.4 %collective-permute-start.1 = (bf16[2,320,256]{2,1,0:T(8,128)(2,1)S(1)}, bf16[2,320,256]{2,1,0:T(8,128)(2,1)}, u32[]{:S(2)}, u32[]{:S(2)}) collective-permute-start(bf16[2,320,256]{2,1,0:T(8,128)(2,1)S(1)} %get-tuple-element.43), channel_id=1, source_target_pairs={{1,2},{2,1},{5,6},{6,5},{9,10},{10,9},{13,14},{14,13},{17,18},{18,... | collective-permute-start | bytes 983048 | tf_op jit(solution)/shard_map/ppermute | solution.py:868
  15.1 1.9 %collective-permute-done.2.refs_3_ = bf16[2,320,256]{2,1,0:T(8,128)(2,1)} collective-permute-done((bf16[2,320,256]{2,1,0:T(8,128)(2,1)S(1)}, bf16[2,320,256]{2,1,0:T(8,128)(2,1)}, u32[]{:S(2)}, u32[]{:S(2)}) %collective-permute-start.2) | collective-permute-done | bytes 327712 | tf_op jit(solution)/shard_map/ppermute | solution.py:868
  17.0 13.8 %shard_map.255 = (bf16[2816,1024]{1,0:T(8,128)(2,1)}, bf16[2816,2048]{1,0:T(8,128)(2,1)}, f32[2816,256]{1,0:T(8,128)}, bf16[106,2,128,256]{3,2,1,0:T(8,128)(2,1)}, bf16[2816,256]{1,0:T(8,128)(2,1)}) custom-call(s32[74]{0:T(128)} %copy-done.1, s32[1]{0:T(128)} %bitcast.refs_1_, bf16[2,512,256]{2,1,0:T(8,128)(2,1)} %refs_2_.2, ...), custom_call_target="tpu_custom_call" | custom-call | flops 12884901888 | bytes 8388608 | tf_op jit(solution)/shard_map/pallas_call | solution.py:739
  30.9 38.1 %shard_map.256 = (bf16[8,144,256]{2,1,0:T(8,128)(2,1)}, bf16[8,144,256]{2,1,0:T(8,128)(2,1)}, bf16[8,128,256]{2,1,0:T(8,128)(2,1)}, bf16[8,128,256]{2,1,0:T(8,12...) custom-call(s32[74]{0:T(128)} %copy-done.1, s32[1]{0:T(128)} %bitcast.refs_1_, ...), custom_call_target="tpu_custom_call" | custom-call | flops 64424509440 | bytes 8388608 | tf_op jit(solution)/shard_map/pallas_call | solution.py:739
  69.6 1.7 %collective-permute-done.6 = bf16[8,144,256]{2,1,0:T(8,128)(2,1)S(1)} collective-permute-done((bf16[8,144,256]{2,1,0:T(8,128)(2,1)}, bf16[8,144,256]{2,1,0:T(8,128)(2,1)S(1)}, u32[]{:S(2)}, u32[]{:S(2)}) %collective-permute-start.6) | collective-permute-done | bytes 589856 | tf_op jit(solution)/shard_map/ppermute | solution.py:890
  72.5 1.9 %collective-permute-start.7 = (bf16[4,144,256]{2,1,0:T(8,128)(2,1)S(1)}, bf16[4,144,256]{2,1,0:T(8,128)(2,1)S(1)}, u32[]{:S(2)}, u32[]{:S(2)}) collective-permute-start(bf16[4,144,256]{2,1,0:T(8,128)(2,1)S(1)} %get-tuple-element.77), channel_id=1, source_target_pairs={{0,8},{4,12},{8,0},{12,4},{16,24},{20,28},{24,16},{28,20},{1,9},{5... | collective-permute-start | bytes 884744 | tf_op jit(solution)/shard_map/ppermute | solution.py:890
  75.7 5.1 %shard_map.257 = (bf16[2,2,512,256]{3,2,1,0:T(8,128)(2,1)S(1)}, bf16[2,2,320,256]{3,2,1,0:T(8,128)(2,1)S(1)}, bf16[2,2,320,256]{3,2,1,0:T(8,128)(2,1)S(1)}) custom-call(s32[74]{0:T(128)S(1)} %copy-done.2, s32[1]{0:T(128)} %bitcast.refs_1_, bf16[2816,256]{1,0:T(8,128)(2,1)S(1)} %copy-done.3, bf16[2816,256]{1,0:T(8,128)(2,1)S(1)} %copy-done.4), custom_call_target="tpu_custom_call" | custom-call | flops 2147483648 | bytes 8388608 | tf_op jit(solution)/shard_map/pallas_call | solution.py:739
  84.3 3.4 %collective-permute-done.8 = bf16[2,144,256]{2,1,0:T(8,128)(2,1)S(1)} collective-permute-done((bf16[2,144,256]{2,1,0:T(8,128)(2,1)S(1)}, bf16[2,144,256]{2,1,0:T(8,128)(2,1)S(1)}, u32[]{:S(2)}, u32[]{:S(2)}) %collective-permute-start.8) | collective-permute-done | bytes 147488 | tf_op jit(solution)/shard_map/ppermute | solution.py:890
  87.8 3.2 %collective-permute-start.9 = (bf16[1,144,256]{2,1,0:T(8,128)(2,1)S(1)}, bf16[1,144,256]{2,1,0:T(8,128)(2,1)S(1)}, u32[]{:S(2)}, u32[]{:S(2)}) collective-permute-start(bf16[1,144,256]{2,1,0:T(8,128)(2,1)S(1)} %add_convert_fusion.10), channel_id=1, source_target_pairs={{0,1},{1,0},{2,3},{3,2},{4,5},{5,4},{6,7},{7,6},{8,9},{9,8},{10,11... | collective-permute-start | bytes 221192 | tf_op jit(solution)/shard_map/ppermute | solution.py:890
  91.3 2.0 %collective-permute-done.9 = bf16[1,144,256]{2,1,0:T(8,128)(2,1)S(1)} collective-permute-done((bf16[1,144,256]{2,1,0:T(8,128)(2,1)S(1)}, bf16[1,144,256]{2,1,0:T(8,128)(2,1)S(1)}, u32[]{:S(2)}, u32[]{:S(2)}) %collective-permute-start.9) | collective-permute-done | bytes 73760 | tf_op jit(solution)/shard_map/ppermute | solution.py:890
  93.3 1.9 %collective-permute-start.10 = (bf16[1,144,256]{2,1,0:T(8,128)(2,1)S(1)}, bf16[1,144,256]{2,1,0:T(8,128)(2,1)S(1)}, u32[]{:S(2)}, u32[]{:S(2)}) collective-permute-start(bf16[1,144,256]{2,1,0:T(8,128)(2,1)S(1)} %add_convert_fusion.9), channel_id=1, source_target_pairs={{0,2},{1,3},{2,0},{3,1},{4,6},{5,7},{6,4},{7,5},{8,10},{9,11},{10,... | collective-permute-start | bytes 221192 | tf_op jit(solution)/shard_map/ppermute | solution.py:890
  95.7 1.5 %collective-permute-start.19 = (bf16[1,128,256]{2,1,0:T(8,128)(2,1)S(1)}, bf16[1,128,256]{2,1,0:T(8,128)(2,1)S(1)}, u32[]{:S(2)}, u32[]{:S(2)}) collective-permute-start(bf16[1,128,256]{2,1,0:T(8,128)(2,1)S(1)} %add_convert_fusion.13), channel_id=1, source_target_pairs={{0,2},{1,3},{2,0},{3,1},{4,6},{5,7},{6,4},{7,5},{8,10},{9,11},{10,... | collective-permute-start | bytes 196616 | tf_op jit(solution)/shard_map/ppermute | solution.py:890
  97.1 1.7 %collective-permute-done.10 = bf16[1,144,256]{2,1,0:T(8,128)(2,1)S(1)} collective-permute-done((bf16[1,144,256]{2,1,0:T(8,128)(2,1)S(1)}, bf16[1,144,256]{2,1,0:T(8,128)(2,1)S(1)}, u32[]{:S(2)}, u32[]{:S(2)}) %collective-permute-start.10) | collective-permute-done | bytes 73760 | tf_op jit(solution)/shard_map/ppermute | solution.py:890
  98.9 2.3 %collective-permute-start.11 = (bf16[1,144,256]{2,1,0:T(8,128)(2,1)S(1)}, bf16[1,144,256]{2,1,0:T(8,128)(2,1)S(1)}, u32[]{:S(2)}, u32[]{:S(2)}) collective-permute-start(bf16[1,144,256]{2,1,0:T(8,128)(2,1)S(1)} %add_convert_fusion.8), channel_id=1, source_target_pairs={{0,1},{1,0},{2,3},{3,2},{4,5},{5,4},{6,7},{7,6},{8,9},{9,8},{10,11... | collective-permute-start | bytes 221192 | tf_op jit(solution)/shard_map/ppermute | solution.py:890
  103.5 1.5 %collective-permute-start.12 = (bf16[2,144,256]{2,1,0:T(8,128)(2,1)S(1)}, bf16[2,144,256]{2,1,0:T(8,128)(2,1)S(1)}, u32[]{:S(2)}, u32[]{:S(2)}) collective-permute-start(bf16[2,144,256]{2,1,0:T(8,128)(2,1)S(1)} %pad_maximum_fusion.4), channel_id=1, source_target_pairs={{0,16},{4,20},{8,24},{12,28},{16,0},{20,4},{24,8},{28,12},{1,17},{... | collective-permute-start | bytes 442376 | tf_op jit(solution)/shard_map/ppermute | solution.py:890
  105.8 2.8 %collective-permute-start.4 = (bf16[2,2,320,256]{3,2,1,0:T(8,128)(2,1)S(1)}, bf16[2,2,320,256]{3,2,1,0:T(8,128)(2,1)S(1)}, u32[]{:S(2)}, u32[]{:S(2)}) collective-permute-start(bf16[2,2,320,256]{3,2,1,0:T(8,128)(2,1)S(1)} %get-tuple-element.75), channel_id=1, source_target_pairs={{0,1},{1,0},{2,3},{3,2},{4,5},{5,4},{6,7},{7,6},{8,9},{9,8},{10,11... | collective-permute-start | bytes 1966088 | tf_op jit(solution)/shard_map/ppermute | solution.py:868
  108.6 1.7 %collective-permute-start.21 = (bf16[2,128,256]{2,1,0:T(8,128)(2,1)S(1)}, bf16[2,128,256]{2,1,0:T(8,128)(2,1)S(1)}, u32[]{:S(2)}, u32[]{:S(2)}) collective-permute-start(bf16[2,128,256]{2,1,0:T(8,128)(2,1)S(1)} %pad_maximum_fusion.5), channel_id=1, source_target_pairs={{0,8},{4,12},{8,0},{12,4},{16,24},{20,28},{24,16},{28,20},{1,9},{5... | collective-permute-start | bytes 393224 | tf_op jit(solution)/shard_map/ppermute | solution.py:890
  110.8 2.8 %collective-permute-done.21 = bf16[2,128,256]{2,1,0:T(8,128)(2,1)S(1)} collective-permute-done((bf16[2,128,256]{2,1,0:T(8,128)(2,1)S(1)}, bf16[2,128,256]{2,1,0:T(8,128)(2,1)S(1)}, u32[]{:S(2)}, u32[]{:S(2)}) %collective-permute-start.21) | collective-permute-done | bytes 131104 | tf_op jit(solution)/shard_map/ppermute | solution.py:890
  114.9 2.1 %collective-permute-done.13 = bf16[4,144,256]{2,1,0:T(8,128)(2,1)S(1)} collective-permute-done((bf16[4,144,256]{2,1,0:T(8,128)(2,1)S(1)}, bf16[4,144,256]{2,1,0:T(8,128)(2,1)S(1)}, u32[]{:S(2)}, u32[]{:S(2)}) %collective-permute-start.13) | collective-permute-done | bytes 294944 | tf_op jit(solution)/shard_map/ppermute | solution.py:890
  117.2 2.9 %collective-permute-done.22 = bf16[4,128,256]{2,1,0:T(8,128)(2,1)S(1)} collective-permute-done((bf16[4,128,256]{2,1,0:T(8,128)(2,1)S(1)}, bf16[4,128,256]{2,1,0:T(8,128)(2,1)S(1)}, u32[]{:S(2)}, u32[]{:S(2)}) %collective-permute-start.22) | collective-permute-done | bytes 262176 | tf_op jit(solution)/shard_map/ppermute | solution.py:890
  120.3 1.3 %fusion.5 = (bf16[2,512,256]{2,1,0:T(8,128)(2,1)}, bf16[2,512,256]{2,1,0:T(8,128)(2,1)}) fusion(bf16[2,2,320,256]{3,2,1,0:T(8,128)(2,1)S(1)} %get-tuple-element.73, bf16[2,2,320,256]{3,2,1,0:T(8,128)(2,1)S(1)} %get-tuple-element.72, bf16[2,2,512,256]{3,2,1,0:T(8,128)(2,1)S(1)} %get-tuple-element.51), kind=kLoop, calls=%fused_computation.16 | loop fusion | flops 3145728 | bytes 3407872 | tf_op jit(solution)/shard_map/add | solution.py:1091
  122.1 3.4 %shard_map.258 = (f32[2,256,768]{2,1,0:T(8,128)}, f32[2,512]{1,0:T(2,128)}, f32[2,256,256]{2,1,0:T(8,128)}, f32[2,256]{1,0:T(2,128)}, f32[2,256]{1,0:T(2,128)}, ...) custom-call(s32[74]{0:T(128)S(1)} %copy-done.2, ...), custom_call_target="tpu_custom_call" | custom-call | flops 1073741824 | bytes 8388608 | tf_op jit(solution)/shard_map/pallas_call | solution.py:739
  (62 shorter events, 17.7 us)
Async XLA Ops:
  1.8 13.3 %collective-permute-start.3 = (bf16[2,320,256]{2,1,0:T(8,128)(2,1)S(1)}, bf16[2,320,256]{2,1,0:T(8,128)(2,1)S(1)}, u32[]{:S(2)}, u32[]{:S(2)}) collective-permute-start(bf16[2,320,256]{2,1,0:T(8,128)(2,1)S(1)} %get-tuple-element.84), channel_id=1, source_target_pairs={{1,2},{2,1},{5,6},{6,5},{9,10},{10,9},{13,14},{14,13},{17,18},{18,... | collective-permute-start | bytes 983048 | tf_op jit(solution)/shard_map/ppermute | solution.py:868
  2.5 14.6 %collective-permute-start.2 = (bf16[2,320,256]{2,1,0:T(8,128)(2,1)S(1)}, bf16[2,320,256]{2,1,0:T(8,128)(2,1)}, u32[]{:S(2)}, u32[]{:S(2)}) collective-permute-start(bf16[2,320,256]{2,1,0:T(8,128)(2,1)S(1)} %get-tuple-element.85), channel_id=1, source_target_pairs={{0,1},{1,0},{2,3},{3,2},{4,5},{5,4},{6,7},{7,6},{8,9},{9,8},{10,11... | collective-permute-start | bytes 983048 | tf_op jit(solution)/shard_map/ppermute | solution.py:868
  13.5 17.4 %collective-permute-start = (bf16[2,320,256]{2,1,0:T(8,128)(2,1)S(1)}, bf16[2,320,256]{2,1,0:T(8,128)(2,1)}, u32[]{:S(2)}, u32[]{:S(2)}) collective-permute-start(bf16[2,320,256]{2,1,0:T(8,128)(2,1)S(1)} %get-tuple-element.42), channel_id=1, source_target_pairs={{0,1},{1,0},{2,3},{3,2},{4,5},{5,4},{6,7},{7,6},{8,9},{9,8},{10,11... | collective-permute-start | bytes 983048 | tf_op jit(solution)/shard_map/ppermute | solution.py:868
  13.7 17.2 %collective-permute-start.1 = (bf16[2,320,256]{2,1,0:T(8,128)(2,1)S(1)}, bf16[2,320,256]{2,1,0:T(8,128)(2,1)}, u32[]{:S(2)}, u32[]{:S(2)}) collective-permute-start(bf16[2,320,256]{2,1,0:T(8,128)(2,1)S(1)} %get-tuple-element.43), channel_id=1, source_target_pairs={{1,2},{2,1},{5,6},{6,5},{9,10},{10,9},{13,14},{14,13},{17,18},{18,... | collective-permute-start | bytes 983048 | tf_op jit(solution)/shard_map/ppermute | solution.py:868
  69.0 2.3 %collective-permute-start.6 = (bf16[8,144,256]{2,1,0:T(8,128)(2,1)}, bf16[8,144,256]{2,1,0:T(8,128)(2,1)S(1)}, u32[]{:S(2)}, u32[]{:S(2)}) collective-permute-start(bf16[8,144,256]{2,1,0:T(8,128)(2,1)} %get-tuple-element.55), channel_id=1, source_target_pairs={{0,4},{4,0},{8,12},{12,8},{16,20},{20,16},{24,28},{28,24},{1,5},{5... | collective-permute-start | bytes 1769480 | tf_op jit(solution)/shard_map/ppermute | solution.py:890
  69.1 5.3 %collective-permute-start.15 = (bf16[8,128,256]{2,1,0:T(8,128)(2,1)}, bf16[8,128,256]{2,1,0:T(8,128)(2,1)S(1)}, u32[]{:S(2)}, u32[]{:S(2)}) collective-permute-start(bf16[8,128,256]{2,1,0:T(8,128)(2,1)} %get-tuple-element.57), channel_id=1, source_target_pairs={{0,4},{4,0},{8,12},{12,8},{16,20},{20,16},{24,28},{28,24},{1,5},{5... | collective-permute-start | bytes 1572872 | tf_op jit(solution)/shard_map/ppermute | solution.py:890
  72.5 9.4 %collective-permute-start.7 = (bf16[4,144,256]{2,1,0:T(8,128)(2,1)S(1)}, bf16[4,144,256]{2,1,0:T(8,128)(2,1)S(1)}, u32[]{:S(2)}, u32[]{:S(2)}) collective-permute-start(bf16[4,144,256]{2,1,0:T(8,128)(2,1)S(1)} %get-tuple-element.77), channel_id=1, source_target_pairs={{0,8},{4,12},{8,0},{12,4},{16,24},{20,28},{24,16},{28,20},{1,9},{5... | collective-permute-start | bytes 884744 | tf_op jit(solution)/shard_map/ppermute | solution.py:890
  75.5 8.4 %collective-permute-start.16 = (bf16[4,128,256]{2,1,0:T(8,128)(2,1)S(1)}, bf16[4,128,256]{2,1,0:T(8,128)(2,1)S(1)}, u32[]{:S(2)}, u32[]{:S(2)}) collective-permute-start(bf16[4,128,256]{2,1,0:T(8,128)(2,1)S(1)} %get-tuple-element.79), channel_id=1, source_target_pairs={{0,16},{4,20},{8,24},{12,28},{16,0},{20,4},{24,8},{28,12},{1,17},{... | collective-permute-start | bytes 786440 | tf_op jit(solution)/shard_map/ppermute | solution.py:890
  82.0 5.8 %collective-permute-start.8 = (bf16[2,144,256]{2,1,0:T(8,128)(2,1)S(1)}, bf16[2,144,256]{2,1,0:T(8,128)(2,1)S(1)}, u32[]{:S(2)}, u32[]{:S(2)}) collective-permute-start(bf16[2,144,256]{2,1,0:T(8,128)(2,1)S(1)} %get-tuple-element.81), channel_id=1, source_target_pairs={{0,16},{4,20},{8,24},{12,28},{16,0},{20,4},{24,8},{28,12},{1,17},{... | collective-permute-start | bytes 442376 | tf_op jit(solution)/shard_map/ppermute | solution.py:890
  84.0 7.0 %collective-permute-start.17 = (bf16[2,128,256]{2,1,0:T(8,128)(2,1)S(1)}, bf16[2,128,256]{2,1,0:T(8,128)(2,1)S(1)}, u32[]{:S(2)}, u32[]{:S(2)}) collective-permute-start(bf16[2,128,256]{2,1,0:T(8,128)(2,1)S(1)} %get-tuple-element.83), channel_id=1, source_target_pairs={{0,8},{4,12},{8,0},{12,4},{16,24},{20,28},{24,16},{28,20},{1,9},{5... | collective-permute-start | bytes 393224 | tf_op jit(solution)/shard_map/ppermute | solution.py:890
  87.8 5.5 %collective-permute-start.9 = (bf16[1,144,256]{2,1,0:T(8,128)(2,1)S(1)}, bf16[1,144,256]{2,1,0:T(8,128)(2,1)S(1)}, u32[]{:S(2)}, u32[]{:S(2)}) collective-permute-start(bf16[1,144,256]{2,1,0:T(8,128)(2,1)S(1)} %add_convert_fusion.10), channel_id=1, source_target_pairs={{0,1},{1,0},{2,3},{3,2},{4,5},{5,4},{6,7},{7,6},{8,9},{9,8},{10,11... | collective-permute-start | bytes 221192 | tf_op jit(solution)/shard_map/ppermute | solution.py:890
  90.9 4.7 %collective-permute-start.18 = (bf16[1,128,256]{2,1,0:T(8,128)(2,1)S(1)}, bf16[1,128,256]{2,1,0:T(8,128)(2,1)S(1)}, u32[]{:S(2)}, u32[]{:S(2)}) collective-permute-start(bf16[1,128,256]{2,1,0:T(8,128)(2,1)S(1)} %add_convert_fusion.14), channel_id=1, source_target_pairs={{0,1},{1,0},{2,3},{3,2},{4,5},{5,4},{6,7},{7,6},{8,9},{9,8},{10,11... | collective-permute-start | bytes 196616 | tf_op jit(solution)/shard_map/ppermute | solution.py:890
  93.3 5.6 %collective-permute-start.10 = (bf16[1,144,256]{2,1,0:T(8,128)(2,1)S(1)}, bf16[1,144,256]{2,1,0:T(8,128)(2,1)S(1)}, u32[]{:S(2)}, u32[]{:S(2)}) collective-permute-start(bf16[1,144,256]{2,1,0:T(8,128)(2,1)S(1)} %add_convert_fusion.9), channel_id=1, source_target_pairs={{0,2},{1,3},{2,0},{3,1},{4,6},{5,7},{6,4},{7,5},{8,10},{9,11},{10,... | collective-permute-start | bytes 221192 | tf_op jit(solution)/shard_map/ppermute | solution.py:890
  95.7 6.1 %collective-permute-start.19 = (bf16[1,128,256]{2,1,0:T(8,128)(2,1)S(1)}, bf16[1,128,256]{2,1,0:T(8,128)(2,1)S(1)}, u32[]{:S(2)}, u32[]{:S(2)}) collective-permute-start(bf16[1,128,256]{2,1,0:T(8,128)(2,1)S(1)} %add_convert_fusion.13), channel_id=1, source_target_pairs={{0,2},{1,3},{2,0},{3,1},{4,6},{5,7},{6,4},{7,5},{8,10},{9,11},{10,... | collective-permute-start | bytes 196616 | tf_op jit(solution)/shard_map/ppermute | solution.py:890
  98.9 4.6 %collective-permute-start.11 = (bf16[1,144,256]{2,1,0:T(8,128)(2,1)S(1)}, bf16[1,144,256]{2,1,0:T(8,128)(2,1)S(1)}, u32[]{:S(2)}, u32[]{:S(2)}) collective-permute-start(bf16[1,144,256]{2,1,0:T(8,128)(2,1)S(1)} %add_convert_fusion.8), channel_id=1, source_target_pairs={{0,1},{1,0},{2,3},{3,2},{4,5},{5,4},{6,7},{7,6},{8,9},{9,8},{10,11... | collective-permute-start | bytes 221192 | tf_op jit(solution)/shard_map/ppermute | solution.py:890
  101.8 6.8 %collective-permute-start.20 = (bf16[1,128,256]{2,1,0:T(8,128)(2,1)S(1)}, bf16[1,128,256]{2,1,0:T(8,128)(2,1)S(1)}, u32[]{:S(2)}, u32[]{:S(2)}) collective-permute-start(bf16[1,128,256]{2,1,0:T(8,128)(2,1)S(1)} %add_convert_fusion.12), channel_id=1, source_target_pairs={{0,1},{1,0},{2,3},{3,2},{4,5},{5,4},{6,7},{7,6},{8,9},{9,8},{10,11... | collective-permute-start | bytes 196616 | tf_op jit(solution)/shard_map/ppermute | solution.py:890
  103.5 6.7 %collective-permute-start.12 = (bf16[2,144,256]{2,1,0:T(8,128)(2,1)S(1)}, bf16[2,144,256]{2,1,0:T(8,128)(2,1)S(1)}, u32[]{:S(2)}, u32[]{:S(2)}) collective-permute-start(bf16[2,144,256]{2,1,0:T(8,128)(2,1)S(1)} %pad_maximum_fusion.4), channel_id=1, source_target_pairs={{0,16},{4,20},{8,24},{12,28},{16,0},{20,4},{24,8},{28,12},{1,17},{... | collective-permute-start | bytes 442376 | tf_op jit(solution)/shard_map/ppermute | solution.py:890
  105.1 15.1 %collective-permute-start.5 = (bf16[2,2,320,256]{3,2,1,0:T(8,128)(2,1)S(1)}, bf16[2,2,320,256]{3,2,1,0:T(8,128)(2,1)S(1)}, u32[]{:S(2)}, u32[]{:S(2)}) collective-permute-start(bf16[2,2,320,256]{3,2,1,0:T(8,128)(2,1)S(1)} %get-tuple-element.74), channel_id=1, source_target_pairs={{1,2},{2,1},{5,6},{6,5},{9,10},{10,9},{13,14},{14,13},{17,18},{18,... | collective-permute-start | bytes 1966088 | tf_op jit(solution)/shard_map/ppermute | solution.py:868
  105.8 14.4 %collective-permute-start.4 = (bf16[2,2,320,256]{3,2,1,0:T(8,128)(2,1)S(1)}, bf16[2,2,320,256]{3,2,1,0:T(8,128)(2,1)S(1)}, u32[]{:S(2)}, u32[]{:S(2)}) collective-permute-start(bf16[2,2,320,256]{3,2,1,0:T(8,128)(2,1)S(1)} %get-tuple-element.75), channel_id=1, source_target_pairs={{0,1},{1,0},{2,3},{3,2},{4,5},{5,4},{6,7},{7,6},{8,9},{9,8},{10,11... | collective-permute-start | bytes 1966088 | tf_op jit(solution)/shard_map/ppermute | solution.py:868
  108.6 5.0 %collective-permute-start.21 = (bf16[2,128,256]{2,1,0:T(8,128)(2,1)S(1)}, bf16[2,128,256]{2,1,0:T(8,128)(2,1)S(1)}, u32[]{:S(2)}, u32[]{:S(2)}) collective-permute-start(bf16[2,128,256]{2,1,0:T(8,128)(2,1)S(1)} %pad_maximum_fusion.5), channel_id=1, source_target_pairs={{0,8},{4,12},{8,0},{12,4},{16,24},{20,28},{24,16},{28,20},{1,9},{5... | collective-permute-start | bytes 393224 | tf_op jit(solution)/shard_map/ppermute | solution.py:890
  110.3 6.8 %collective-permute-start.13 = (bf16[4,144,256]{2,1,0:T(8,128)(2,1)S(1)}, bf16[4,144,256]{2,1,0:T(8,128)(2,1)S(1)}, u32[]{:S(2)}, u32[]{:S(2)}) collective-permute-start(bf16[4,144,256]{2,1,0:T(8,128)(2,1)S(1)} %pad_maximum_fusion.2), channel_id=1, source_target_pairs={{0,8},{4,12},{8,0},{12,4},{16,24},{20,28},{24,16},{28,20},{1,9},{5... | collective-permute-start | bytes 884744 | tf_op jit(solution)/shard_map/ppermute | solution.py:890
  113.6 6.4 %collective-permute-start.22 = (bf16[4,128,256]{2,1,0:T(8,128)(2,1)S(1)}, bf16[4,128,256]{2,1,0:T(8,128)(2,1)S(1)}, u32[]{:S(2)}, u32[]{:S(2)}) collective-permute-start(bf16[4,128,256]{2,1,0:T(8,128)(2,1)S(1)} %pad_maximum_fusion.3), channel_id=1, source_target_pairs={{0,16},{4,20},{8,24},{12,28},{16,0},{20,4},{24,8},{28,12},{1,17},{... | collective-permute-start | bytes 786440 | tf_op jit(solution)/shard_map/ppermute | solution.py:890
  117.1 5.0 %collective-permute-start.14 = (bf16[8,144,256]{2,1,0:T(8,128)(2,1)S(1)}, bf16[8,144,256]{2,1,0:T(8,128)(2,1)S(1)}, u32[]{:S(2)}, u32[]{:S(2)}) collective-permute-start(bf16[8,144,256]{2,1,0:T(8,128)(2,1)S(1)} %pad_maximum_fusion.refs_1_), channel_id=1, source_target_pairs={{0,4},{4,0},{8,12},{12,8},{16,20},{20,16},{24,28},{28,24},{1,5},{5... | collective-permute-start | bytes 1769480 | tf_op jit(solution)/shard_map/ppermute | solution.py:890
  120.1 2.0 %collective-permute-start.23 = (bf16[8,128,256]{2,1,0:T(8,128)(2,1)S(1)}, bf16[8,128,256]{2,1,0:T(8,128)(2,1)S(1)}, u32[]{:S(2)}, u32[]{:S(2)}) collective-permute-start(bf16[8,128,256]{2,1,0:T(8,128)(2,1)S(1)} %pad_maximum_fusion.1.refs_3_), channel_id=1, source_target_pairs={{0,4},{4,0},{8,12},{12,8},{16,20},{20,16},{24,28},{28,24},{1,5},{5... | collective-permute-start | bytes 1572872 | tf_op jit(solution)/shard_map/ppermute | solution.py:890
  (6 other events, 23.2 us)

commit v3 on v2

--- a/solution.py
+++ b/solution.py
@@ -99,17 +99,20 @@
 
     def over_groups(self, most, visit):
         def one(d):
-            size = jnp.maximum(self.size(d), 2)
-            after = self.size(d + 1)
-            two = (size == 2) & (after >= 1) & (after <= 2)
-
-            @pl.when(two)
+            size, after = self.size(d), self.size(d + 1)
+            two = (size <= 2) & (after >= 1) & (after <= 2)
+
+            @pl.when(two & (size == 1))
+            def _():
+                visit([(d, 1), (d + 1, 2)])
+
+            @pl.when(two & (size == 2))
             def _():
                 visit([(d, 2), (d + 1, 2)])
 
             for n in range(2, most + 1):
 
-                @pl.when((size == n) & jnp.logical_not(two))
+                @pl.when((jnp.maximum(size, 2) == n) & jnp.logical_not(two))
                 def _():
                     visit([(d, n)])
 
@@ -764,7 +767,7 @@
             r.spent[row * base + doc] = spent
             if doc < DOCS:
                 size = starts[doc + 1] - starts[doc]
-                spent = spent + size + 180
+                spent = spent + size + jnp.where(size > QB, 180, 130)
                 spent = spent + jnp.where(size > 2 * QB, 160, 0) + jnp.where(size > 3 * QB, 190, 0)
         for section in range(1, sections):
             low, high = jnp.int32(0), jnp.int32(0)
@@ -820,20 +823,21 @@
     low, high = (low // base, low % base), (high // base, high % base)
     table = r.table
     carry = (jnp.int32(0), jnp.int32(0), jnp.int32(0))
-    for kind in range(2, whole // QB + 1):
+    for kind in range(1, whole // QB + 1):
         for row in range(2):
 
             def one(doc, carry):
                 k, offset, tile = carry
                 begin = r.start[row * base + doc]
                 length = r.start[row * base + doc + 1] - begin
-                blocks = jnp.maximum(lax.shift_right_logical(length + (QB - 1), 7), 2)
+                blocks = lax.shift_right_logical(length + (QB - 1), 7)
                 table[k] = begin - place * whole + REACH + row * span
                 table[ROOM + k] = length
                 table[2 * ROOM + k] = offset
                 table[3 * ROOM + k] = tile
                 taken = (blocks == kind).astype(jnp.int32)
                 offset = offset + taken * lax.bitwise_and(length + 15, -16)
+                blocks = jnp.maximum(blocks, 2)
                 return k + taken, offset, tile + taken * blocks * blocks
 
             carry = lax.fori_loop(low[row], high[row], one, carry)

time: 127 us -> 127 us (level); the launches traced: 126 us -> 124 us
  Pallas kernels: 63 us -> 59.9 us
  starting transfers between devices: 30.5 us -> 32 us
    pallas_call x5, Pallas kernels: 63 us -> 59.9 us  [call(): pl.pallas_call(run, out_shape=[jax.ShapeDtypeStruct(s, d) for s, d, _ in...]
  transfers between devices with their start and end apart: 24 -> 24, of which waited for: 14 -> 11; matrix products, arithmetic and copies ran while one was open for 4% -> 4% of each run, Pallas kernels for 17% -> 17%
where the time goes in v3:
time: 127 us; the launch traced here: 124 us
  Pallas kernels  59.9 us (47%)
  starting transfers between devices  32 us (25%)
  waiting for transfers between devices  23.4 us (18%)
  other arithmetic  6.59 us (5%)
    pallas_call x5, Pallas kernels, call(): pl.pallas_call(run, out_shape=[jax.ShapeDtypeStruct(s, d) for s, d, _ in...  59.9 us
    ppermute x18, waiting for transfers between devices, exchange(): return lax.ppermute(value, axis, [(i, i ^ stride) for i in range(count)])  21.1 us
    ppermute x18, starting transfers between devices, exchange(): return lax.ppermute(value, axis, [(i, i ^ stride) for i in range(count)])  19.5 us
    ppermute x6, starting transfers between devices, halo(): lax.ppermute(value, 'pipe', [p for i, j in pairs for p in ((i, j), (j, i))])  12.6 us
    convert_element_type x10, other arithmetic, added(): return (a.astype(F32) + b.astype(F32)).astype(BF)  2.66 us
  transfers between devices with their start and end apart: 24, of which 11 were waited for; matrix products, arithmetic and copies ran while one was open for 4% of the time, Pallas kernels for 17%

profile of v3, /device:TPU:0, one launch (start us, length us, event | category | flops | bytes accessed | tf_op | source)
XLA Modules:
  0.0 124.3 jit_solution(669554743407269195)
XLA Ops:
  2.5 5.9 %collective-permute-start.2 = (bf16[2,320,256]{2,1,0:T(8,128)(2,1)S(1)}, bf16[2,320,256]{2,1,0:T(8,128)(2,1)}, u32[]{:S(2)}, u32[]{:S(2)}) collective-permute-start(bf16[2,320,256]{2,1,0:T(8,128)(2,1)S(1)} %get-tuple-element.85), channel_id=1, source_target_pairs={{0,1},{1,0},{2,3},{3,2},{4,5},{5,4},{6,7},{7,6},{8,9},{9,8},{10,11... | collective-permute-start | bytes 983048 | tf_op jit(solution)/shard_map/ppermute | solution.py:872
  9.1 2.0 %shard_map.254.refs_0_ = s32[74]{0:T(128)S(1)} custom-call(s32[2,2048]{1,0:T(2,128)S(1)} %copy-done, s32[1]{0:T(128)} %bitcast.refs_1_, s32[1]{0:T(128)} %bitcast.1.refs_2_), custom_call_target="tpu_custom_call" | custom-call | flops 1048576 | bytes 8388608 | tf_op jit(solution)/shard_map/pallas_call | solution.py:742
  12.8 1.4 %collective-permute-start.1 = (bf16[2,320,256]{2,1,0:T(8,128)(2,1)S(1)}, bf16[2,320,256]{2,1,0:T(8,128)(2,1)}, u32[]{:S(2)}, u32[]{:S(2)}) collective-permute-start(bf16[2,320,256]{2,1,0:T(8,128)(2,1)S(1)} %get-tuple-element.43), channel_id=1, source_target_pairs={{1,2},{2,1},{5,6},{6,5},{9,10},{10,9},{13,14},{14,13},{17,18},{18,... | collective-permute-start | bytes 983048 | tf_op jit(solution)/shard_map/ppermute | solution.py:872
  14.2 2.3 %collective-permute-done.2.refs_3_ = bf16[2,320,256]{2,1,0:T(8,128)(2,1)} collective-permute-done((bf16[2,320,256]{2,1,0:T(8,128)(2,1)S(1)}, bf16[2,320,256]{2,1,0:T(8,128)(2,1)}, u32[]{:S(2)}, u32[]{:S(2)}) %collective-permute-start.2) | collective-permute-done | bytes 327712 | tf_op jit(solution)/shard_map/ppermute | solution.py:872
  16.5 13.4 %shard_map.255 = (bf16[2816,1024]{1,0:T(8,128)(2,1)}, bf16[2816,2048]{1,0:T(8,128)(2,1)}, f32[2816,256]{1,0:T(8,128)}, bf16[106,2,128,256]{3,2,1,0:T(8,128)(2,1)}, bf16[2816,256]{1,0:T(8,128)(2,1)}) custom-call(s32[74]{0:T(128)} %copy-done.1, s32[1]{0:T(128)} %bitcast.refs_1_, bf16[2,512,256]{2,1,0:T(8,128)(2,1)} %refs_2_.2, ...), custom_call_target="tpu_custom_call" | custom-call | flops 12884901888 | bytes 8388608 | tf_op jit(solution)/shard_map/pallas_call | solution.py:742
  29.9 35.9 %shard_map.256 = (bf16[8,144,256]{2,1,0:T(8,128)(2,1)}, bf16[8,144,256]{2,1,0:T(8,128)(2,1)}, bf16[8,128,256]{2,1,0:T(8,128)(2,1)}, bf16[8,128,256]{2,1,0:T(8,12...) custom-call(s32[74]{0:T(128)} %copy-done.1, s32[1]{0:T(128)} %bitcast.refs_1_, ...), custom_call_target="tpu_custom_call" | custom-call | flops 64424509440 | bytes 8388608 | tf_op jit(solution)/shard_map/pallas_call | solution.py:742
  66.4 1.7 %collective-permute-done.6 = bf16[8,144,256]{2,1,0:T(8,128)(2,1)S(1)} collective-permute-done((bf16[8,144,256]{2,1,0:T(8,128)(2,1)}, bf16[8,144,256]{2,1,0:T(8,128)(2,1)S(1)}, u32[]{:S(2)}, u32[]{:S(2)}) %collective-permute-start.6) | collective-permute-done | bytes 589856 | tf_op jit(solution)/shard_map/ppermute | solution.py:894
  70.6 3.2 %collective-permute-start.16 = (bf16[4,128,256]{2,1,0:T(8,128)(2,1)S(1)}, bf16[4,128,256]{2,1,0:T(8,128)(2,1)S(1)}, u32[]{:S(2)}, u32[]{:S(2)}) collective-permute-start(bf16[4,128,256]{2,1,0:T(8,128)(2,1)S(1)} %get-tuple-element.79), channel_id=1, source_target_pairs={{0,16},{4,20},{8,24},{12,28},{16,0},{20,4},{24,8},{28,12},{1,17},{... | collective-permute-start | bytes 786440 | tf_op jit(solution)/shard_map/ppermute | solution.py:894
  73.9 5.4 %shard_map.257 = (bf16[2,2,512,256]{3,2,1,0:T(8,128)(2,1)S(1)}, bf16[2,2,320,256]{3,2,1,0:T(8,128)(2,1)S(1)}, bf16[2,2,320,256]{3,2,1,0:T(8,128)(2,1)S(1)}) custom-call(s32[74]{0:T(128)S(1)} %copy-done.2, s32[1]{0:T(128)} %bitcast.refs_1_, bf16[2816,256]{1,0:T(8,128)(2,1)S(1)} %copy-done.3, bf16[2816,256]{1,0:T(8,128)(2,1)S(1)} %copy-done.4), custom_call_target="tpu_custom_call" | custom-call | flops 2147483648 | bytes 8388608 | tf_op jit(solution)/shard_map/pallas_call | solution.py:742
  79.3 1.4 %collective-permute-start.8 = (bf16[2,144,256]{2,1,0:T(8,128)(2,1)S(1)}, bf16[2,144,256]{2,1,0:T(8,128)(2,1)S(1)}, u32[]{:S(2)}, u32[]{:S(2)}) collective-permute-start(bf16[2,144,256]{2,1,0:T(8,128)(2,1)S(1)} %get-tuple-element.81), channel_id=1, source_target_pairs={{0,16},{4,20},{8,24},{12,28},{16,0},{20,4},{24,8},{28,12},{1,17},{... | collective-permute-start | bytes 442376 | tf_op jit(solution)/shard_map/ppermute | solution.py:894
  82.0 2.8 %collective-permute-done.8 = bf16[2,144,256]{2,1,0:T(8,128)(2,1)S(1)} collective-permute-done((bf16[2,144,256]{2,1,0:T(8,128)(2,1)S(1)}, bf16[2,144,256]{2,1,0:T(8,128)(2,1)S(1)}, u32[]{:S(2)}, u32[]{:S(2)}) %collective-permute-start.8) | collective-permute-done | bytes 147488 | tf_op jit(solution)/shard_map/ppermute | solution.py:894
  84.8 2.0 %collective-permute-start.9 = (bf16[1,144,256]{2,1,0:T(8,128)(2,1)S(1)}, bf16[1,144,256]{2,1,0:T(8,128)(2,1)S(1)}, u32[]{:S(2)}, u32[]{:S(2)}) collective-permute-start(bf16[1,144,256]{2,1,0:T(8,128)(2,1)S(1)} %add_convert_fusion.10), channel_id=1, source_target_pairs={{0,1},{1,0},{2,3},{3,2},{4,5},{5,4},{6,7},{7,6},{8,9},{9,8},{10,11... | collective-permute-start | bytes 221192 | tf_op jit(solution)/shard_map/ppermute | solution.py:894
  86.8 1.6 %collective-permute-start.18 = (bf16[1,128,256]{2,1,0:T(8,128)(2,1)S(1)}, bf16[1,128,256]{2,1,0:T(8,128)(2,1)S(1)}, u32[]{:S(2)}, u32[]{:S(2)}) collective-permute-start(bf16[1,128,256]{2,1,0:T(8,128)(2,1)S(1)} %add_convert_fusion.14), channel_id=1, source_target_pairs={{0,1},{1,0},{2,3},{3,2},{4,5},{5,4},{6,7},{7,6},{8,9},{9,8},{10,11... | collective-permute-start | bytes 196616 | tf_op jit(solution)/shard_map/ppermute | solution.py:894
  89.4 3.7 %collective-permute-start.10 = (bf16[1,144,256]{2,1,0:T(8,128)(2,1)S(1)}, bf16[1,144,256]{2,1,0:T(8,128)(2,1)S(1)}, u32[]{:S(2)}, u32[]{:S(2)}) collective-permute-start(bf16[1,144,256]{2,1,0:T(8,128)(2,1)S(1)} %add_convert_fusion.9), channel_id=1, source_target_pairs={{0,2},{1,3},{2,0},{3,1},{4,6},{5,7},{6,4},{7,5},{8,10},{9,11},{10,... | collective-permute-start | bytes 221192 | tf_op jit(solution)/shard_map/ppermute | solution.py:894
  94.2 2.5 %collective-permute-done.10 = bf16[1,144,256]{2,1,0:T(8,128)(2,1)S(1)} collective-permute-done((bf16[1,144,256]{2,1,0:T(8,128)(2,1)S(1)}, bf16[1,144,256]{2,1,0:T(8,128)(2,1)S(1)}, u32[]{:S(2)}, u32[]{:S(2)}) %collective-permute-start.10) | collective-permute-done | bytes 73760 | tf_op jit(solution)/shard_map/ppermute | solution.py:894
  96.7 2.1 %collective-permute-done.19 = bf16[1,128,256]{2,1,0:T(8,128)(2,1)S(1)} collective-permute-done((bf16[1,128,256]{2,1,0:T(8,128)(2,1)S(1)}, bf16[1,128,256]{2,1,0:T(8,128)(2,1)S(1)}, u32[]{:S(2)}, u32[]{:S(2)}) %collective-permute-start.19) | collective-permute-done | bytes 65568 | tf_op jit(solution)/shard_map/ppermute | solution.py:894
  99.2 1.9 %collective-permute-done.11 = bf16[1,144,256]{2,1,0:T(8,128)(2,1)S(1)} collective-permute-done((bf16[1,144,256]{2,1,0:T(8,128)(2,1)S(1)}, bf16[1,144,256]{2,1,0:T(8,128)(2,1)S(1)}, u32[]{:S(2)}, u32[]{:S(2)}) %collective-permute-start.11) | collective-permute-done | bytes 73760 | tf_op jit(solution)/shard_map/ppermute | solution.py:894
  101.1 1.5 %collective-permute-start.12 = (bf16[2,144,256]{2,1,0:T(8,128)(2,1)S(1)}, bf16[2,144,256]{2,1,0:T(8,128)(2,1)S(1)}, u32[]{:S(2)}, u32[]{:S(2)}) collective-permute-start(bf16[2,144,256]{2,1,0:T(8,128)(2,1)S(1)} %pad_maximum_fusion.4), channel_id=1, source_target_pairs={{0,16},{4,20},{8,24},{12,28},{16,0},{20,4},{24,8},{28,12},{1,17},{... | collective-permute-start | bytes 442376 | tf_op jit(solution)/shard_map/ppermute | solution.py:894
  103.4 3.8 %collective-permute-start.4 = (bf16[2,2,320,256]{3,2,1,0:T(8,128)(2,1)S(1)}, bf16[2,2,320,256]{3,2,1,0:T(8,128)(2,1)S(1)}, u32[]{:S(2)}, u32[]{:S(2)}) collective-permute-start(bf16[2,2,320,256]{3,2,1,0:T(8,128)(2,1)S(1)} %get-tuple-element.75), channel_id=1, source_target_pairs={{0,1},{1,0},{2,3},{3,2},{4,5},{5,4},{6,7},{7,6},{8,9},{9,8},{10,11... | collective-permute-start | bytes 1966088 | tf_op jit(solution)/shard_map/ppermute | solution.py:872
  109.4 2.8 %collective-permute-done.21 = bf16[2,128,256]{2,1,0:T(8,128)(2,1)S(1)} collective-permute-done((bf16[2,128,256]{2,1,0:T(8,128)(2,1)S(1)}, bf16[2,128,256]{2,1,0:T(8,128)(2,1)S(1)}, u32[]{:S(2)}, u32[]{:S(2)}) %collective-permute-start.21) | collective-permute-done | bytes 131104 | tf_op jit(solution)/shard_map/ppermute | solution.py:894
  112.7 2.6 %collective-permute-done.13 = bf16[4,144,256]{2,1,0:T(8,128)(2,1)S(1)} collective-permute-done((bf16[4,144,256]{2,1,0:T(8,128)(2,1)S(1)}, bf16[4,144,256]{2,1,0:T(8,128)(2,1)S(1)}, u32[]{:S(2)}, u32[]{:S(2)}) %collective-permute-start.13) | collective-permute-done | bytes 294944 | tf_op jit(solution)/shard_map/ppermute | solution.py:894
  115.5 3.2 %collective-permute-done.22 = bf16[4,128,256]{2,1,0:T(8,128)(2,1)S(1)} collective-permute-done((bf16[4,128,256]{2,1,0:T(8,128)(2,1)S(1)}, bf16[4,128,256]{2,1,0:T(8,128)(2,1)S(1)}, u32[]{:S(2)}, u32[]{:S(2)}) %collective-permute-start.22) | collective-permute-done | bytes 262176 | tf_op jit(solution)/shard_map/ppermute | solution.py:894
  118.9 1.3 %fusion.5 = (bf16[2,512,256]{2,1,0:T(8,128)(2,1)}, bf16[2,512,256]{2,1,0:T(8,128)(2,1)}) fusion(bf16[2,2,320,256]{3,2,1,0:T(8,128)(2,1)S(1)} %get-tuple-element.73, bf16[2,2,320,256]{3,2,1,0:T(8,128)(2,1)S(1)} %get-tuple-element.72, bf16[2,2,512,256]{3,2,1,0:T(8,128)(2,1)S(1)} %get-tuple-element.51), kind=kLoop, calls=%fused_computation.16 | loop fusion | flops 3145728 | bytes 3407872 | tf_op jit(solution)/shard_map/add | solution.py:1095
  120.7 3.4 %shard_map.258 = (f32[2,256,768]{2,1,0:T(8,128)}, f32[2,512]{1,0:T(2,128)}, f32[2,256,256]{2,1,0:T(8,128)}, f32[2,256]{1,0:T(2,128)}, f32[2,256]{1,0:T(2,128)}, ...) custom-call(s32[74]{0:T(128)S(1)} %copy-done.2, ...), custom_call_target="tpu_custom_call" | custom-call | flops 1073741824 | bytes 8388608 | tf_op jit(solution)/shard_map/pallas_call | solution.py:742
  (62 shorter events, 15.7 us)
Async XLA Ops:
  1.8 12.4 %collective-permute-start.3 = (bf16[2,320,256]{2,1,0:T(8,128)(2,1)S(1)}, bf16[2,320,256]{2,1,0:T(8,128)(2,1)S(1)}, u32[]{:S(2)}, u32[]{:S(2)}) collective-permute-start(bf16[2,320,256]{2,1,0:T(8,128)(2,1)S(1)} %get-tuple-element.84), channel_id=1, source_target_pairs={{1,2},{2,1},{5,6},{6,5},{9,10},{10,9},{13,14},{14,13},{17,18},{18,... | collective-permute-start | bytes 983048 | tf_op jit(solution)/shard_map/ppermute | solution.py:872
  2.5 14.0 %collective-permute-start.2 = (bf16[2,320,256]{2,1,0:T(8,128)(2,1)S(1)}, bf16[2,320,256]{2,1,0:T(8,128)(2,1)}, u32[]{:S(2)}, u32[]{:S(2)}) collective-permute-start(bf16[2,320,256]{2,1,0:T(8,128)(2,1)S(1)} %get-tuple-element.85), channel_id=1, source_target_pairs={{0,1},{1,0},{2,3},{3,2},{4,5},{5,4},{6,7},{7,6},{8,9},{9,8},{10,11... | collective-permute-start | bytes 983048 | tf_op jit(solution)/shard_map/ppermute | solution.py:872
  12.7 17.2 %collective-permute-start = (bf16[2,320,256]{2,1,0:T(8,128)(2,1)S(1)}, bf16[2,320,256]{2,1,0:T(8,128)(2,1)}, u32[]{:S(2)}, u32[]{:S(2)}) collective-permute-start(bf16[2,320,256]{2,1,0:T(8,128)(2,1)S(1)} %get-tuple-element.42), channel_id=1, source_target_pairs={{0,1},{1,0},{2,3},{3,2},{4,5},{5,4},{6,7},{7,6},{8,9},{9,8},{10,11... | collective-permute-start | bytes 983048 | tf_op jit(solution)/shard_map/ppermute | solution.py:872
  12.8 17.1 %collective-permute-start.1 = (bf16[2,320,256]{2,1,0:T(8,128)(2,1)S(1)}, bf16[2,320,256]{2,1,0:T(8,128)(2,1)}, u32[]{:S(2)}, u32[]{:S(2)}) collective-permute-start(bf16[2,320,256]{2,1,0:T(8,128)(2,1)S(1)} %get-tuple-element.43), channel_id=1, source_target_pairs={{1,2},{2,1},{5,6},{6,5},{9,10},{10,9},{13,14},{14,13},{17,18},{18,... | collective-permute-start | bytes 983048 | tf_op jit(solution)/shard_map/ppermute | solution.py:872
  65.8 2.3 %collective-permute-start.6 = (bf16[8,144,256]{2,1,0:T(8,128)(2,1)}, bf16[8,144,256]{2,1,0:T(8,128)(2,1)S(1)}, u32[]{:S(2)}, u32[]{:S(2)}) collective-permute-start(bf16[8,144,256]{2,1,0:T(8,128)(2,1)} %get-tuple-element.55), channel_id=1, source_target_pairs={{0,4},{4,0},{8,12},{12,8},{16,20},{20,16},{24,28},{28,24},{1,5},{5... | collective-permute-start | bytes 1769480 | tf_op jit(solution)/shard_map/ppermute | solution.py:894
  65.9 3.6 %collective-permute-start.15 = (bf16[8,128,256]{2,1,0:T(8,128)(2,1)}, bf16[8,128,256]{2,1,0:T(8,128)(2,1)S(1)}, u32[]{:S(2)}, u32[]{:S(2)}) collective-permute-start(bf16[8,128,256]{2,1,0:T(8,128)(2,1)} %get-tuple-element.57), channel_id=1, source_target_pairs={{0,4},{4,0},{8,12},{12,8},{16,20},{20,16},{24,28},{28,24},{1,5},{5... | collective-permute-start | bytes 1572872 | tf_op jit(solution)/shard_map/ppermute | solution.py:894
  69.3 9.9 %collective-permute-start.7 = (bf16[4,144,256]{2,1,0:T(8,128)(2,1)S(1)}, bf16[4,144,256]{2,1,0:T(8,128)(2,1)S(1)}, u32[]{:S(2)}, u32[]{:S(2)}) collective-permute-start(bf16[4,144,256]{2,1,0:T(8,128)(2,1)S(1)} %get-tuple-element.77), channel_id=1, source_target_pairs={{0,8},{4,12},{8,0},{12,4},{16,24},{20,28},{24,16},{28,20},{1,9},{5... | collective-permute-start | bytes 884744 | tf_op jit(solution)/shard_map/ppermute | solution.py:894
  70.6 10.1 %collective-permute-start.16 = (bf16[4,128,256]{2,1,0:T(8,128)(2,1)S(1)}, bf16[4,128,256]{2,1,0:T(8,128)(2,1)S(1)}, u32[]{:S(2)}, u32[]{:S(2)}) collective-permute-start(bf16[4,128,256]{2,1,0:T(8,128)(2,1)S(1)} %get-tuple-element.79), channel_id=1, source_target_pairs={{0,16},{4,20},{8,24},{12,28},{16,0},{20,4},{24,8},{28,12},{1,17},{... | collective-permute-start | bytes 786440 | tf_op jit(solution)/shard_map/ppermute | solution.py:894
  79.3 5.4 %collective-permute-start.8 = (bf16[2,144,256]{2,1,0:T(8,128)(2,1)S(1)}, bf16[2,144,256]{2,1,0:T(8,128)(2,1)S(1)}, u32[]{:S(2)}, u32[]{:S(2)}) collective-permute-start(bf16[2,144,256]{2,1,0:T(8,128)(2,1)S(1)} %get-tuple-element.81), channel_id=1, source_target_pairs={{0,16},{4,20},{8,24},{12,28},{16,0},{20,4},{24,8},{28,12},{1,17},{... | collective-permute-start | bytes 442376 | tf_op jit(solution)/shard_map/ppermute | solution.py:894
  80.8 5.9 %collective-permute-start.17 = (bf16[2,128,256]{2,1,0:T(8,128)(2,1)S(1)}, bf16[2,128,256]{2,1,0:T(8,128)(2,1)S(1)}, u32[]{:S(2)}, u32[]{:S(2)}) collective-permute-start(bf16[2,128,256]{2,1,0:T(8,128)(2,1)S(1)} %get-tuple-element.83), channel_id=1, source_target_pairs={{0,8},{4,12},{8,0},{12,4},{16,24},{20,28},{24,16},{28,20},{1,9},{5... | collective-permute-start | bytes 393224 | tf_op jit(solution)/shard_map/ppermute | solution.py:894
  84.8 4.6 %collective-permute-start.9 = (bf16[1,144,256]{2,1,0:T(8,128)(2,1)S(1)}, bf16[1,144,256]{2,1,0:T(8,128)(2,1)S(1)}, u32[]{:S(2)}, u32[]{:S(2)}) collective-permute-start(bf16[1,144,256]{2,1,0:T(8,128)(2,1)S(1)} %add_convert_fusion.10), channel_id=1, source_target_pairs={{0,1},{1,0},{2,3},{3,2},{4,5},{5,4},{6,7},{7,6},{8,9},{9,8},{10,11... | collective-permute-start | bytes 221192 | tf_op jit(solution)/shard_map/ppermute | solution.py:894
  86.8 6.3 %collective-permute-start.18 = (bf16[1,128,256]{2,1,0:T(8,128)(2,1)S(1)}, bf16[1,128,256]{2,1,0:T(8,128)(2,1)S(1)}, u32[]{:S(2)}, u32[]{:S(2)}) collective-permute-start(bf16[1,128,256]{2,1,0:T(8,128)(2,1)S(1)} %add_convert_fusion.14), channel_id=1, source_target_pairs={{0,1},{1,0},{2,3},{3,2},{4,5},{5,4},{6,7},{7,6},{8,9},{9,8},{10,11... | collective-permute-start | bytes 196616 | tf_op jit(solution)/shard_map/ppermute | solution.py:894
  89.4 7.2 %collective-permute-start.10 = (bf16[1,144,256]{2,1,0:T(8,128)(2,1)S(1)}, bf16[1,144,256]{2,1,0:T(8,128)(2,1)S(1)}, u32[]{:S(2)}, u32[]{:S(2)}) collective-permute-start(bf16[1,144,256]{2,1,0:T(8,128)(2,1)S(1)} %add_convert_fusion.9), channel_id=1, source_target_pairs={{0,2},{1,3},{2,0},{3,1},{4,6},{5,7},{6,4},{7,5},{8,10},{9,11},{10,... | collective-permute-start | bytes 221192 | tf_op jit(solution)/shard_map/ppermute | solution.py:894
  93.1 5.7 %collective-permute-start.19 = (bf16[1,128,256]{2,1,0:T(8,128)(2,1)S(1)}, bf16[1,128,256]{2,1,0:T(8,128)(2,1)S(1)}, u32[]{:S(2)}, u32[]{:S(2)}) collective-permute-start(bf16[1,128,256]{2,1,0:T(8,128)(2,1)S(1)} %add_convert_fusion.13), channel_id=1, source_target_pairs={{0,2},{1,3},{2,0},{3,1},{4,6},{5,7},{6,4},{7,5},{8,10},{9,11},{10,... | collective-permute-start | bytes 196616 | tf_op jit(solution)/shard_map/ppermute | solution.py:894
  96.6 4.4 %collective-permute-start.11 = (bf16[1,144,256]{2,1,0:T(8,128)(2,1)S(1)}, bf16[1,144,256]{2,1,0:T(8,128)(2,1)S(1)}, u32[]{:S(2)}, u32[]{:S(2)}) collective-permute-start(bf16[1,144,256]{2,1,0:T(8,128)(2,1)S(1)} %add_convert_fusion.8), channel_id=1, source_target_pairs={{0,1},{1,0},{2,3},{3,2},{4,5},{5,4},{6,7},{7,6},{8,9},{9,8},{10,11... | collective-permute-start | bytes 221192 | tf_op jit(solution)/shard_map/ppermute | solution.py:894
  98.8 8.4 %collective-permute-start.20 = (bf16[1,128,256]{2,1,0:T(8,128)(2,1)S(1)}, bf16[1,128,256]{2,1,0:T(8,128)(2,1)S(1)}, u32[]{:S(2)}, u32[]{:S(2)}) collective-permute-start(bf16[1,128,256]{2,1,0:T(8,128)(2,1)S(1)} %add_convert_fusion.12), channel_id=1, source_target_pairs={{0,1},{1,0},{2,3},{3,2},{4,5},{5,4},{6,7},{7,6},{8,9},{9,8},{10,11... | collective-permute-start | bytes 196616 | tf_op jit(solution)/shard_map/ppermute | solution.py:894
  101.1 7.1 %collective-permute-start.12 = (bf16[2,144,256]{2,1,0:T(8,128)(2,1)S(1)}, bf16[2,144,256]{2,1,0:T(8,128)(2,1)S(1)}, u32[]{:S(2)}, u32[]{:S(2)}) collective-permute-start(bf16[2,144,256]{2,1,0:T(8,128)(2,1)S(1)} %pad_maximum_fusion.4), channel_id=1, source_target_pairs={{0,16},{4,20},{8,24},{12,28},{16,0},{20,4},{24,8},{28,12},{1,17},{... | collective-permute-start | bytes 442376 | tf_op jit(solution)/shard_map/ppermute | solution.py:894
  102.7 16.2 %collective-permute-start.5 = (bf16[2,2,320,256]{3,2,1,0:T(8,128)(2,1)S(1)}, bf16[2,2,320,256]{3,2,1,0:T(8,128)(2,1)S(1)}, u32[]{:S(2)}, u32[]{:S(2)}) collective-permute-start(bf16[2,2,320,256]{3,2,1,0:T(8,128)(2,1)S(1)} %get-tuple-element.74), channel_id=1, source_target_pairs={{1,2},{2,1},{5,6},{6,5},{9,10},{10,9},{13,14},{14,13},{17,18},{18,... | collective-permute-start | bytes 1966088 | tf_op jit(solution)/shard_map/ppermute | solution.py:872
  103.4 15.5 %collective-permute-start.4 = (bf16[2,2,320,256]{3,2,1,0:T(8,128)(2,1)S(1)}, bf16[2,2,320,256]{3,2,1,0:T(8,128)(2,1)S(1)}, u32[]{:S(2)}, u32[]{:S(2)}) collective-permute-start(bf16[2,2,320,256]{3,2,1,0:T(8,128)(2,1)S(1)} %get-tuple-element.75), channel_id=1, source_target_pairs={{0,1},{1,0},{2,3},{3,2},{4,5},{5,4},{6,7},{7,6},{8,9},{9,8},{10,11... | collective-permute-start | bytes 1966088 | tf_op jit(solution)/shard_map/ppermute | solution.py:872
  107.2 5.0 %collective-permute-start.21 = (bf16[2,128,256]{2,1,0:T(8,128)(2,1)S(1)}, bf16[2,128,256]{2,1,0:T(8,128)(2,1)S(1)}, u32[]{:S(2)}, u32[]{:S(2)}) collective-permute-start(bf16[2,128,256]{2,1,0:T(8,128)(2,1)S(1)} %pad_maximum_fusion.5), channel_id=1, source_target_pairs={{0,8},{4,12},{8,0},{12,4},{16,24},{20,28},{24,16},{28,20},{1,9},{5... | collective-permute-start | bytes 393224 | tf_op jit(solution)/shard_map/ppermute | solution.py:894
  108.2 7.2 %collective-permute-start.13 = (bf16[4,144,256]{2,1,0:T(8,128)(2,1)S(1)}, bf16[4,144,256]{2,1,0:T(8,128)(2,1)S(1)}, u32[]{:S(2)}, u32[]{:S(2)}) collective-permute-start(bf16[4,144,256]{2,1,0:T(8,128)(2,1)S(1)} %pad_maximum_fusion.2), channel_id=1, source_target_pairs={{0,8},{4,12},{8,0},{12,4},{16,24},{20,28},{24,16},{28,20},{1,9},{5... | collective-permute-start | bytes 884744 | tf_op jit(solution)/shard_map/ppermute | solution.py:894
  112.3 6.4 %collective-permute-start.22 = (bf16[4,128,256]{2,1,0:T(8,128)(2,1)S(1)}, bf16[4,128,256]{2,1,0:T(8,128)(2,1)S(1)}, u32[]{:S(2)}, u32[]{:S(2)}) collective-permute-start(bf16[4,128,256]{2,1,0:T(8,128)(2,1)S(1)} %pad_maximum_fusion.3), channel_id=1, source_target_pairs={{0,16},{4,20},{8,24},{12,28},{16,0},{20,4},{24,8},{28,12},{1,17},{... | collective-permute-start | bytes 786440 | tf_op jit(solution)/shard_map/ppermute | solution.py:894
  115.4 5.3 %collective-permute-start.14 = (bf16[8,144,256]{2,1,0:T(8,128)(2,1)S(1)}, bf16[8,144,256]{2,1,0:T(8,128)(2,1)S(1)}, u32[]{:S(2)}, u32[]{:S(2)}) collective-permute-start(bf16[8,144,256]{2,1,0:T(8,128)(2,1)S(1)} %pad_maximum_fusion.refs_1_), channel_id=1, source_target_pairs={{0,4},{4,0},{8,12},{12,8},{16,20},{20,16},{24,28},{28,24},{1,5},{5... | collective-permute-start | bytes 1769480 | tf_op jit(solution)/shard_map/ppermute | solution.py:894
  118.7 2.0 %collective-permute-start.23 = (bf16[8,128,256]{2,1,0:T(8,128)(2,1)S(1)}, bf16[8,128,256]{2,1,0:T(8,128)(2,1)S(1)}, u32[]{:S(2)}, u32[]{:S(2)}) collective-permute-start(bf16[8,128,256]{2,1,0:T(8,128)(2,1)S(1)} %pad_maximum_fusion.1.refs_3_), channel_id=1, source_target_pairs={{0,4},{4,0},{8,12},{12,8},{16,20},{20,16},{24,28},{28,24},{1,5},{5... | collective-permute-start | bytes 1572872 | tf_op jit(solution)/shard_map/ppermute | solution.py:894
  (6 other events, 27.8 us)
